TPU v7x, 32 devices: a whole 2x2x4 slice. The times are simulated.
32 devices in a mesh: lat: 16 (over z, y, x), lon: 2 (over core).
Axes of the slice: x: 2, y: 2, z: 4, core: 2. Of those that a mesh axis runs over, the one named last changes fastest.
Arguments:
- velocity: float32 [2, 8, 128, 256], P(None, None, 'lat', 'lon'), may hold values from -1.8 to 1.8
- thickness: float32 [8, 128, 256], P(None, 'lat', 'lon'), may hold values from 0.5 to 1.5
- hydrography: float32 [2, 8, 128, 256], P(None, None, 'lat', 'lon'), may hold values from -6 to 6
- tracers: float32 [17, 8, 128, 256], P(None, None, 'lat', 'lon'), may hold values from -6 to 6
- land_mask: int32 [128, 256], P('lat', 'lon'), may hold values 0 or 1
- bottom_layer: int32 [128, 256], P('lat', 'lon'), may hold values from 1 to 8
- row_biome: int32 [128], P('lat'), may hold values from 0 to 3
- reaction_rates: float32 [17, 17], replicated, may hold values from -0.75 to 0.75
- growth_rates: float32 [4], replicated, may hold values from 0.2 to 2
Outputs:
- new_velocity: float32 [2, 8, 128, 256], P(None, None, 'lat', 'lon')
- new_thickness: float32 [8, 128, 256], P(None, 'lat', 'lon')
- new_hydrography: float32 [2, 8, 128, 256], P(None, None, 'lat', 'lon')
- new_tracers: float32 [17, 8, 128, 256], P(None, None, 'lat', 'lon')
- absorbed: float32 [8, 128, 256], P(None, 'lat', 'lon')
All inputs are finite; a program needn't handle non-finite values. No bound on the sum of `land_mask` on one device may be relied on, other than what follows from the above.
Results may differ from a plain program's by a relative error of at most 0.0003.
Values sent between devices are 32-bit elements; how exact they have to be, the bound alone decides.
A program may use at most 64 MiB of HBM per device.

v0:
```python
import jax
import jax.numpy as jnp
from jax import lax
from jax.sharding import PartitionSpec as P

NSUB = 2


heat_coef = 0.2
salt_coef = 0.25
gravity = 0.3
viscosity = 0.1
coriolis_coef = 0.3
tracer_diff = 0.1
kappa_base = 0.02
kappa_var = 0.1
water_att = 0.1
chlorophyll_att = 0.2
heat_gain = 1.0


def with_halo(cells, sides, width):
    for axis, dim in sides:
        count = lax.axis_size(axis)
        ends = count - 1
        head = lax.slice_in_dim(cells, 0, width, axis=dim)
        tail = lax.slice_in_dim(cells, cells.shape[dim] - width, cells.shape[dim], axis=dim)
        cells = jnp.concatenate(
            [
                lax.ppermute(tail, axis, [(i, (i + 1) % count) for i in range(ends)]),
                cells,
                lax.ppermute(head, axis, [((i + 1) % count, i) for i in range(ends)]),
            ],
            axis=dim,
        )
    return cells


def shifted(values, step_rows, step_cols):
    leading = [(0, 0)] * (values.ndim - 2)
    padded = jnp.pad(values, leading + [(1, 1), (1, 1)])
    height_span = values.shape[-2]
    width_span = values.shape[-1]
    return padded[
        ..., 1 + step_rows : 1 + step_rows + height_span, 1 + step_cols : 1 + step_cols + width_span
    ]


def trimmed(values, margin):
    if margin == 0:
        return values
    return values[..., margin:-margin, margin:-margin]


def face_masks(wet_cells):
    return (wet_cells * shifted(wet_cells, 0, 1), wet_cells * shifted(wet_cells, 1, 0))


def laplace(values, wet_east, wet_north):
    east_flux = wet_east * (shifted(values, 0, 1) - values)
    north_flux = wet_north * (shifted(values, 1, 0) - values)
    return east_flux - shifted(east_flux, 0, -1) + north_flux - shifted(north_flux, -1, 0)


def wet_layers(floor_depth, layers):
    layer_height = lax.broadcasted_iota(jnp.float32, (layers, 1, 1), 0)
    return (layer_height < floor_depth[None]).astype(jnp.float32)


def latitude_rows(start, count, total_rows):
    positions = start + lax.broadcasted_iota(jnp.float32, (count, 1), 0)
    return 2.0 * (positions + 0.5) / total_rows - 1.0


def density_of(hydrography):
    return salt_coef * hydrography[1] - heat_coef * hydrography[0]


def momentum(velocity, thickness, hydrography, wet_cells, coriolis):
    flow_east = velocity[0]
    flow_north = velocity[1]
    wet_east, wet_north = face_masks(wet_cells)
    pressure = gravity * thickness + density_of(hydrography)
    new_east = wet_east * (
        flow_east
        + coriolis * flow_north
        - (shifted(pressure, 0, 1) - pressure)
        + viscosity * laplace(flow_east, wet_east, wet_north)
    )
    new_north = wet_north * (
        flow_north
        - coriolis * flow_east
        - (shifted(pressure, 1, 0) - pressure)
        + viscosity * laplace(flow_north, wet_east, wet_north)
    )
    volume_east = wet_east * flow_east * 0.5 * (thickness + shifted(thickness, 0, 1))
    volume_north = wet_north * flow_north * 0.5 * (thickness + shifted(thickness, 1, 0))
    new_height = wet_cells * (
        thickness
        - (volume_east - shifted(volume_east, 0, -1) + volume_north - shifted(volume_north, -1, 0))
    )
    return (new_east, new_north, new_height)


def mixing(hydrography, wet_cells):
    density = density_of(hydrography)
    below = jnp.concatenate(
        [density[1:] - density[:-1], jnp.zeros((1,) + density.shape[1:], jnp.float32)], 0
    )
    return wet_cells * (kappa_base + kappa_var / (1.0 + 10.0 * below * below))


def heat_salt(hydrography, wet_cells):
    wet_east, wet_north = face_masks(wet_cells)
    return wet_cells * (hydrography + tracer_diff * laplace(hydrography, wet_east, wet_north))


def light_field(tracers, wet_cells, insolation):
    chlorophyll = tracers[1]
    attenuation = wet_cells * (water_att + chlorophyll_att * chlorophyll * chlorophyll)
    overhead = jnp.cumsum(attenuation, axis=0) - attenuation
    top_light = insolation * jnp.exp(-overhead)
    return (top_light, top_light * (1.0 - jnp.exp(-attenuation)))


def tracer_step(
    tracers,
    flow_east,
    flow_north,
    thickness,
    kappa,
    wet_cells,
    reaction_rates,
    growth_field,
    top_light,
):
    sub_step = 1.0 / NSUB
    wet_east, wet_north = face_masks(wet_cells)
    transport_x = wet_east * flow_east * 0.5 * (thickness + shifted(thickness, 0, 1))
    transport_y = wet_north * flow_north * 0.5 * (thickness + shifted(thickness, 1, 0))
    diffuse_x = wet_east * 0.5 * (kappa + shifted(kappa, 0, 1))
    diffuse_y = wet_north * 0.5 * (kappa + shifted(kappa, 1, 0))
    east_next = shifted(tracers, 0, 1)
    north_next = shifted(tracers, 1, 0)
    flux_x = transport_x * jnp.where(transport_x > 0, tracers, east_next) - diffuse_x * (
        east_next - tracers
    )
    flux_y = transport_y * jnp.where(transport_y > 0, tracers, north_next) - diffuse_y * (
        north_next - tracers
    )
    advected = tracers - sub_step * (
        flux_x - shifted(flux_x, 0, -1) + flux_y - shifted(flux_y, -1, 0)
    )
    flattened = advected.reshape(advected.shape[0], -1)
    coupled = jnp.dot(reaction_rates, flattened, precision=lax.Precision.HIGHEST).reshape(
        advected.shape
    )
    nutrient = advected[0]
    plankton = advected[1]
    uptake = growth_field * top_light * plankton * nutrient * nutrient / (1.0 + nutrient * nutrient)
    change = jnp.concatenate(
        [(coupled[0] - uptake)[None], (coupled[1] + uptake)[None], coupled[2:]], 0
    )
    return wet_cells * (advected + sub_step * change)


def run_substeps(
    spread,
    count,
    flow_east,
    flow_north,
    flow_height,
    flow_kappa,
    wet_flow,
    reaction_rates,
    growth_flow,
    top_light,
):
    for inner_step in range(count):
        stepped = tracer_step(
            spread,
            trimmed(flow_east, inner_step),
            trimmed(flow_north, inner_step),
            trimmed(flow_height, inner_step),
            trimmed(flow_kappa, inner_step),
            trimmed(wet_flow, inner_step),
            reaction_rates,
            trimmed(growth_flow, inner_step),
            trimmed(top_light, inner_step),
        )
        spread = trimmed(stepped, 1)
    return spread


def per_device(
    velocity,
    thickness,
    hydrography,
    tracers,
    land_mask,
    bottom_layer,
    row_biome,
    reaction_rates,
    growth_rates,
):
    kind_count, layers, block_rows, block_cols = tracers.shape
    total_rows = block_rows * lax.axis_size("lat")
    first_row = (lax.axis_index("lat") * block_rows).astype(jnp.float32)
    floor_depth = (land_mask * bottom_layer).astype(jnp.float32)
    biome_table = (
        row_biome[:, None] == lax.broadcasted_iota(jnp.int32, (1, growth_rates.shape[0]), 1)
    ).astype(jnp.float32)
    growth_column = jnp.dot(biome_table, growth_rates[:, None], precision=lax.Precision.HIGHEST)
    growth_plane = jnp.broadcast_to(growth_column, (block_rows, block_cols))
    packed_state = jnp.concatenate(
        [
            velocity.reshape(2 * layers, block_rows, block_cols),
            thickness,
            hydrography.reshape(2 * layers, block_rows, block_cols),
            floor_depth[None],
            growth_plane[None],
        ],
        0,
    )
    rim_width = 2
    dyn_width = 1
    rimmed = with_halo(packed_state, (("lat", 1), ("lon", 2)), dyn_width)
    span_rows = rimmed.shape[1]
    span_cols = rimmed.shape[2]
    old_velocity = rimmed[: 2 * layers].reshape(2, layers, span_rows, span_cols)
    old_height = rimmed[2 * layers : 3 * layers]
    old_hydro = rimmed[3 * layers : 5 * layers].reshape(2, layers, span_rows, span_cols)
    depth_dyn = rimmed[5 * layers]
    wet_dyn = wet_layers(depth_dyn, layers)
    coriolis = coriolis_coef * latitude_rows(first_row - dyn_width, span_rows, total_rows)
    new_east, new_north, new_height = momentum(
        old_velocity, old_height, old_hydro, wet_dyn, coriolis
    )
    kappa_dyn = mixing(old_hydro, wet_dyn)
    mixed = trimmed(
        heat_salt(trimmed(old_hydro, dyn_width - 1), trimmed(wet_dyn, dyn_width - 1)), 1
    )
    packed_flow = jnp.concatenate(
        [
            trimmed(new_east, 1),
            trimmed(new_north, 1),
            trimmed(new_height, 1),
            trimmed(kappa_dyn, 1),
            floor_depth[None],
            growth_plane[None],
        ],
        0,
    )
    flowed = with_halo(packed_flow, (("lat", 1), ("lon", 2)), rim_width)
    flow_east = flowed[:layers]
    flow_north = flowed[layers : 2 * layers]
    flow_height = flowed[2 * layers : 3 * layers]
    flow_kappa = flowed[3 * layers : 4 * layers]
    depth_flow = flowed[4 * layers]
    growth_flow = flowed[4 * layers + 1]
    wet_flow = wet_layers(depth_flow, layers)
    latitude = latitude_rows(first_row - rim_width, block_rows + 2 * rim_width, total_rows)
    insolation = 1.0 - 0.8 * latitude * latitude
    current = tracers
    top_light = None
    absorbed_flow = None
    spread = with_halo(
        current.reshape(kind_count * layers, block_rows, block_cols),
        (("lat", 1), ("lon", 2)),
        rim_width,
    )
    spread = spread.reshape(
        kind_count, layers, block_rows + 2 * rim_width, block_cols + 2 * rim_width
    )
    top_light, absorbed_flow = light_field(spread, wet_flow, insolation)
    current = run_substeps(
        spread,
        rim_width,
        flow_east,
        flow_north,
        flow_height,
        flow_kappa,
        wet_flow,
        reaction_rates,
        growth_flow,
        top_light,
    )
    absorbed = trimmed(absorbed_flow, rim_width)
    new_hydrography = jnp.concatenate([(mixed[0] + heat_gain * absorbed)[None], mixed[1:]], 0)
    new_velocity = jnp.stack([trimmed(flow_east, rim_width), trimmed(flow_north, rim_width)])
    new_thickness = trimmed(flow_height, rim_width)
    return (new_velocity, new_thickness, new_hydrography, current, absorbed)


def solution(mesh):
    in_specs = (
        P(None, None, "lat", "lon"),
        P(None, "lat", "lon"),
        P(None, None, "lat", "lon"),
        P(None, None, "lat", "lon"),
        P("lat", "lon"),
        P("lat", "lon"),
        P("lat"),
        P(),
        P(),
    )
    out_specs = (
        P(None, None, "lat", "lon"),
        P(None, "lat", "lon"),
        P(None, None, "lat", "lon"),
        P(None, None, "lat", "lon"),
        P(None, "lat", "lon"),
    )
    return jax.shard_map(
        per_device, mesh=mesh, in_specs=in_specs, out_specs=out_specs, check_vma=False
    )
```

profile of v0, /device:TPU:8, one launch (start us, length us, event | category | flops | bytes accessed | tf_op | source)
XLA Modules:
  0.0 90.5 jit_solution(382964401826437275)
XLA Ops:
  4.8 4.2 %collective-permute-start.1 = (f32[42,1,128]{2,1,0:T(1,128)S(1)}, f32[42,1,128]{2,1,0:T(1,128)S(1)}, u32[]{:S(2)}, u32[]{:S(2)}) collective-permute-start(f32[42,1,128]{2,1,0:T(1,128)S(1)} %get-tuple-element.72), channel_id=1, source_target_pairs={{2,0},{4,2},{6,4},{8,6},{10,8},{12,10},{14,12},{16,14},{18,16},{20... | collective-permute-start | bytes 64520 | tf_op jit(solution)/shard_map/ppermute | solution.py:32
  9.0 1.9 %collective-permute-start = (f32[42,1,128]{2,1,0:T(1,128)S(1)}, f32[42,1,128]{2,1,0:T(1,128)S(1)}, u32[]{:S(2)}, u32[]{:S(2)}) collective-permute-start(f32[42,1,128]{2,1,0:T(1,128)S(1)} %get-tuple-element.71), channel_id=1, source_target_pairs={{0,2},{2,4},{4,6},{6,8},{8,10},{10,12},{12,14},{14,16},{16,18},{18... | collective-permute-start | bytes 64520 | tf_op jit(solution)/shard_map/ppermute | solution.py:30
  11.0 1.3 %fusion.54 = (f32[136,2,128]{2,1,0:T(2,128)S(1)}, f32[136,2,128]{2,1,0:T(2,128)S(1)}) fusion(f32[136,8,128]{2,1,0:T(8,128)} %bitcast.59), kind=kLoop, calls=%fused_computation.158 | loop fusion | bytes 557056 | tf_op jit(solution)/shard_map/slice | solution.py:27
  12.3 5.7 %collective-permute-start.9 = (f32[136,2,128]{2,1,0:T(2,128)S(1)}, f32[136,2,128]{2,1,0:T(2,128)S(1)}, u32[]{:S(2)}, u32[]{:S(2)}) collective-permute-start(f32[136,2,128]{2,1,0:T(2,128)S(1)} %get-tuple-element.60), channel_id=1, source_target_pairs={{2,0},{4,2},{6,4},{8,6},{10,8},{12,10},{14,12},{16,14},{18,16},{20... | collective-permute-start | bytes 417800 | tf_op jit(solution)/shard_map/ppermute | solution.py:32
  18.0 1.9 %collective-permute-start.8 = (f32[136,2,128]{2,1,0:T(2,128)S(1)}, f32[136,2,128]{2,1,0:T(2,128)S(1)}, u32[]{:S(2)}, u32[]{:S(2)}) collective-permute-start(f32[136,2,128]{2,1,0:T(2,128)S(1)} %get-tuple-element.59), channel_id=1, source_target_pairs={{0,2},{2,4},{4,6},{6,8},{8,10},{10,12},{12,14},{14,16},{16,18},{18... | collective-permute-start | bytes 417800 | tf_op jit(solution)/shard_map/ppermute | solution.py:30
  20.2 1.3 %collective-permute-start.3 = (f32[42,10,1]{2,1,0:T(8,128)S(1)}, f32[42,10,1]{2,1,0:T(8,128)S(1)}, u32[]{:S(2)}, u32[]{:S(2)}) collective-permute-start(f32[42,10,1]{2,1,0:T(8,128)S(1)} %get-tuple-element.62), channel_id=1, source_target_pairs={{1,0},{3,2},{5,4},{7,6},{9,8},{11,10},{13,12},{15,14},{17,16},{19,... | collective-permute-start | bytes 5048 | tf_op jit(solution)/shard_map/ppermute | solution.py:32
  21.5 3.1 %collective-permute-start.2 = (f32[42,10,1]{2,1,0:T(8,128)S(1)}, f32[42,10,1]{2,1,0:T(8,128)S(1)}, u32[]{:S(2)}, u32[]{:S(2)}) collective-permute-start(f32[42,10,1]{2,1,0:T(8,128)S(1)} %get-tuple-element.61), channel_id=1, source_target_pairs={{0,1},{2,3},{4,5},{6,7},{8,9},{10,11},{12,13},{14,15},{16,17},{18,... | collective-permute-start | bytes 5048 | tf_op jit(solution)/shard_map/ppermute | solution.py:30
  24.7 1.1 %collective-permute-done.2 = f32[42,10,1]{2,1,0:T(8,128)S(1)} collective-permute-done((f32[42,10,1]{2,1,0:T(8,128)S(1)}, f32[42,10,1]{2,1,0:T(8,128)S(1)}, u32[]{:S(2)}, u32[]{:S(2)}) %collective-permute-start.2) | collective-permute-done | bytes 1712 | tf_op jit(solution)/shard_map/ppermute | solution.py:30
  28.7 5.7 %collective-permute-start.5 = (f32[34,2,128]{2,1,0:T(2,128)S(1)}, f32[34,2,128]{2,1,0:T(2,128)S(1)}, u32[]{:S(2)}, u32[]{:S(2)}) collective-permute-start(f32[34,2,128]{2,1,0:T(2,128)S(1)} %get-tuple-element.74), channel_id=1, source_target_pairs={{2,0},{4,2},{6,4},{8,6},{10,8},{12,10},{14,12},{16,14},{18,16},{20... | collective-permute-start | bytes 104456 | tf_op jit(solution)/shard_map/ppermute | solution.py:32
  34.4 1.9 %collective-permute-start.4 = (f32[34,2,128]{2,1,0:T(2,128)S(1)}, f32[34,2,128]{2,1,0:T(2,128)S(1)}, u32[]{:S(2)}, u32[]{:S(2)}) collective-permute-start(f32[34,2,128]{2,1,0:T(2,128)S(1)} %get-tuple-element.73), channel_id=1, source_target_pairs={{0,2},{2,4},{4,6},{6,8},{8,10},{10,12},{12,14},{14,16},{16,18},{18... | collective-permute-start | bytes 104456 | tf_op jit(solution)/shard_map/ppermute | solution.py:30
  36.6 5.5 %collective-permute-done.4 = f32[34,2,128]{2,1,0:T(2,128)S(1)} collective-permute-done((f32[34,2,128]{2,1,0:T(2,128)S(1)}, f32[34,2,128]{2,1,0:T(2,128)S(1)}, u32[]{:S(2)}, u32[]{:S(2)}) %collective-permute-start.4) | collective-permute-done | bytes 34848 | tf_op jit(solution)/shard_map/ppermute | solution.py:30
  42.3 1.3 %collective-permute-start.7 = (f32[34,12,2]{2,1,0:T(8,128)S(1)}, f32[34,12,2]{2,1,0:T(8,128)S(1)}, u32[]{:S(2)}, u32[]{:S(2)}) collective-permute-start(f32[34,12,2]{2,1,0:T(8,128)S(1)} %get-tuple-element.66), channel_id=1, source_target_pairs={{1,0},{3,2},{5,4},{7,6},{9,8},{11,10},{13,12},{15,14},{17,16},{19,... | collective-permute-start | bytes 9800 | tf_op jit(solution)/shard_map/ppermute | solution.py:32
  43.6 3.1 %collective-permute-start.6 = (f32[34,12,2]{2,1,0:T(8,128)S(1)}, f32[34,12,2]{2,1,0:T(8,128)S(1)}, u32[]{:S(2)}, u32[]{:S(2)}) collective-permute-start(f32[34,12,2]{2,1,0:T(8,128)S(1)} %get-tuple-element.65), channel_id=1, source_target_pairs={{0,1},{2,3},{4,5},{6,7},{8,9},{10,11},{12,13},{14,15},{16,17},{18,... | collective-permute-start | bytes 9800 | tf_op jit(solution)/shard_map/ppermute | solution.py:30
  50.1 0.9 %broadcast_compare_fusion.2 = (pred[8,10,130]{2,1,0:T(8,128)(4,1)}, f32[8,10,130]{2,1,0:T(8,128)}, pred[8,10,130]{2,1,0:T(8,128)(4,1)}, f32[8,10,130]{2,1,0:T(8,128)}) fusion(f32[8,10,130]{2,1,0:T(8,128)S(1)} %get-tuple-element.55, f32[34,12,132]{2,1,0:T(8,128)S(1)} %pad_maximum_fusion.7, f32[8,10,130]{2,1,0:T(8,128)S(1)} %slice.473), kind=kLoop, calls=%fused_computation.95 | loop fusion | flops 124800 | bytes 270400 | tf_op jit(solution)/shard_map/gt | solution.py:145
  52.9 1.3 %collective-permute-start.11 = (f32[136,12,2]{0,2,1:T(2,128)S(1)}, f32[136,12,2]{0,2,1:T(2,128)S(1)}, u32[]{:S(2)}, u32[]{:S(2)}) collective-permute-start(f32[136,12,2]{0,2,1:T(2,128)S(1)} %copy.15), channel_id=1, source_target_pairs={{1,0},{3,2},{5,4},{7,6},{9,8},{11,10},{13,12},{15,14},{17,16},{19,... | collective-permute-start | bytes 39176 | tf_op jit(solution)/shard_map/ppermute | solution.py:32
  54.7 3.6 %collective-permute-start.10 = (f32[136,12,2]{0,2,1:T(2,128)S(1)}, f32[136,12,2]{0,2,1:T(2,128)}, u32[]{:S(2)}, u32[]{:S(2)}) collective-permute-start(f32[136,12,2]{0,2,1:T(2,128)S(1)} %copy.14), channel_id=1, source_target_pairs={{0,1},{2,3},{4,5},{6,7},{8,9},{10,11},{12,13},{14,15},{16,17},{18,... | collective-permute-start | bytes 39176 | tf_op jit(solution)/shard_map/ppermute | solution.py:30
  58.4 1.9 %add_multiply_fusion.2 = (f32[8,10,130]{2,1,0:T(8,128)}, f32[8,10,130]{2,1,0:T(8,128)}) fusion(f32[8,10,130]{2,1,0:T(8,128)} %get-tuple-element.56, f32[8,10,130]{2,1,0:T(8,128)S(1)} %slice.473), kind=kLoop, calls=%fused_computation.63 | loop fusion | flops 83200 | bytes 166400 | tf_op jit(solution)/shard_map/mul | solution.py:141
  61.6 1.3 %copy.16 = f32[136,12,2]{2,1,0:T(8,128)S(1)} copy(f32[136,12,2]{0,2,1:T(2,128)} %collective-permute-done.10) | data formatting | bytes 26112 | tf_op jit(solution)/shard_map/ppermute | solution.py:30
  63.0 1.5 %pad_maximum_fusion.2 = f32[136,12,132]{2,1,0:T(8,128)S(1)} fusion(f32[136,12,2]{2,1,0:T(8,128)S(1)} %copy.17, f32[136,2,128]{2,1,0:T(2,128)S(1)} %collective-permute-done.9, f32[136,8,128]{2,1,0:T(8,128)S(1)} %bitcast.61, f32[136,2,128]{2,1,0:T(2,128)S(1)} %collective-permute-done.8, f32[136,12,2]{2,1,0:T(8,128)S(1)} %copy.16), kind=kLoop, calls=%fused_computation.7 | loop fusion | flops 861696 | bytes 1723392 | tf_op jit(solution)/shard_map/concatenate | solution.py:28
  65.2 1.2 %multiply_subtract_fusion.5 = (f32[17,8,12,132]{3,2,1,0:T(8,128)S(1)}, f32[17,8,12,132]{3,2,1,0:T(8,128)S(1)}) fusion(f32[17,8,12,132]{3,2,1,0:T(8,128)S(1)} %bitcast.57, f32[8,12,132]{2,1,0:T(8,128)S(1)} %get-tuple-element.63, f32[8,12,132]{2,1,0:T(8,128)S(1)} %get-tuple-element.18, pred[8,12,132]{2,1,0:T(8,128)(4,1)S(1)} %copy-done.15, ...), kind=kLoop, calls=%fused_computation.13 | loop fusion | flops 2154240 | bytes 2813184 | tf_op jit(solution)/shard_map/sub | solution.py:145
  66.5 1.2 %multiply_subtract_fusion.3 = f32[17,8,12,132]{3,2,1,0:T(8,128)S(1)} fusion(f32[17,8,12,132]{3,2,1,0:T(8,128)S(1)} %bitcast.58, f32[17,8,12,132]{3,2,1,0:T(8,128)S(1)} %get-tuple-element.38, f32[17,8,12,132]{3,2,1,0:T(8,128)S(1)} %get-tuple-element.37), kind=kLoop, calls=%fused_computation.11 | loop fusion | flops 1077120 | bytes 3446784 | tf_op jit(solution)/shard_map/sub | solution.py:151
  67.7 1.0 %reshape.132 = f32[17,12672]{1,0:T(8,128)S(1)} reshape(f32[17,8,12,132]{3,2,1,0:T(8,128)S(1)} %multiply_subtract_fusion.3) | data formatting | bytes 1723392 | tf_op jit(solution)/shard_map/reshape | solution.py:154
  68.7 1.2 %convolution_bitcast_fusion = f32[17,12672]{1,0:T(8,128)S(1)} fusion(f32[17,12672]{1,0:T(8,128)S(1)} %reshape.132, f32[17,17]{1,0:T(8,128)S(1)} %copy-done), kind=kOutput, calls=%fused_computation | convolution fusion | flops 43946496 | bytes 1724548 | tf_op jit(solution)/shard_map/dot_general | solution.py:155
  71.0 2.4 %slice.396 = f32[15,8,12,132]{3,2,1,0:T(8,128)} reshape(f32[15,12672]{1,0:T(8,128)S(1)} %slice.482) | data formatting | bytes 1520640 | tf_op jit(solution)/shard_map/slice | solution.py:162
  73.5 1.0 %fusion.45 = (f32[1,8,12,132]{3,2,1,0:T(8,128)S(1)}, f32[1,8,12,132]{3,2,1,0:T(8,128)S(1)}, f32[8,12,132]{2,1,0:T(8,128)S(1)}) fusion(f32[1,8,12,132]{3,2,1,0:T(8,128)} %squeeze.15, f32[17,8,12,132]{3,2,1,0:T(8,128)S(1)} %multiply_subtract_fusion.3, f32[12,132]{1,0:T(8,128)S(1)} %get-tuple-element.47, f32[8,12,132]{2,1,0:T(8,128)S(1)} %copy-done.4, ...), kind=kOutput, calls=%fused_computation.154 | output fusion | flops 228096 | bytes 743936 | tf_op jit(solution)/shard_map/jit(cumsum)/reduce_window_sum | solution.py:121
  74.6 2.9 %fusion = f32[17,8,10,130]{3,2,1,0:T(8,128)S(1)} fusion(f32[17,8,12,132]{3,2,1,0:T(8,128)S(1)} %multiply_subtract_fusion.3, f32[15,8,12,132]{3,2,1,0:T(8,128)} %slice.396, f32[1,8,12,132]{3,2,1,0:T(8,128)S(1)} %add.246, f32[1,8,12,132]{3,2,1,0:T(8,128)S(1)} %get-tuple-element.15, f32[8,10,130]{2,1,0:T(8,128)S(1)} %copy-done.3), kind=kLoop, calls=%fused_computation.3 | loop fusion | flops 884000 | bytes 2317696 | tf_op jit(solution)/shard_map/mul | solution.py:164
  77.6 1.2 %multiply_subtract_fusion.2 = (f32[17,8,10,130]{3,2,1,0:T(8,128)S(1)}, f32[17,8,10,130]{3,2,1,0:T(8,128)S(1)}) fusion(f32[17,8,10,130]{3,2,1,0:T(8,128)S(1)} %fusion, f32[8,10,130]{2,1,0:T(8,128)S(1)} %copy-done.7, f32[8,10,130]{2,1,0:T(8,128)S(1)} %copy-done.5, pred[8,10,130]{2,1,0:T(8,128)(4,1)S(1)} %copy-done.13, f32[8,10,130]{2,1,0:T(8,128)S(1)} %copy-done.8, ...), kind=kLoop, calls=%fused_computation.10 | loop fusion | flops 1768000 | bytes 2308800 | tf_op jit(solution)/shard_map/sub | solution.py:145
  78.9 1.4 %multiply_subtract_fusion = f32[17,8,10,130]{3,2,1,0:T(8,128)S(1)} fusion(f32[17,8,10,130]{3,2,1,0:T(8,128)S(1)} %fusion, f32[17,8,10,130]{3,2,1,0:T(8,128)S(1)} %get-tuple-element.36, f32[17,8,10,130]{3,2,1,0:T(8,128)S(1)} %get-tuple-element.35), kind=kLoop, calls=%fused_computation.8 | loop fusion | flops 884000 | bytes 2828800 | tf_op jit(solution)/shard_map/sub | solution.py:151
  81.1 1.0 %convolution_bitcast_fusion.1 = f32[17,10400]{1,0:T(8,128)S(1)} fusion(f32[17,10400]{1,0:T(8,128)S(1)} %reshape.133, f32[17,17]{1,0:T(8,128)S(1)} %copy-done), kind=kOutput, calls=%fused_computation.1 | convolution fusion | flops 36067200 | bytes 1415556 | tf_op jit(solution)/shard_map/dot_general | solution.py:155
  82.4 1.6 %fusion.31 = (f32[1,8,8,128]{3,2,1,0:T(8,128)S(1)}, f32[8,8,128]{2,1,0:T(8,128)}) fusion(f32[2,8,10,130]{3,2,1,0:T(8,128)} %copy-done.11, f32[8,12,132]{2,1,0:T(8,128)S(1)} %copy-done.4, f32[8,12,132]{2,1,0:T(8,128)S(1)} %get-tuple-element.84), kind=kLoop, calls=%fused_computation.113 | loop fusion | flops 32768 | bytes 163840 | tf_op jit(solution)/shard_map/broadcast_in_dim | solution.py:289
  84.0 2.6 %slice.419 = f32[15,8,10,130]{3,2,1,0:T(8,128)} reshape(f32[15,10400]{1,0:T(8,128)S(1)} %slice.495) | data formatting | bytes 1248000 | tf_op jit(solution)/shard_map/slice | solution.py:162
  87.7 2.8 %fusion.5 = f32[17,8,8,128]{3,2,1,0:T(8,128)} fusion(f32[17,8,10,130]{3,2,1,0:T(8,128)S(1)} %multiply_subtract_fusion, f32[15,8,10,130]{3,2,1,0:T(8,128)} %slice.419, f32[1,8,10,130]{3,2,1,0:T(8,128)S(1)} %add_bitcast_fusion, f32[1,8,10,130]{3,2,1,0:T(8,128)S(1)} %get-tuple-element.9, f32[8,8,128]{2,1,0:T(8,128)S(1)} %copy-done.12), kind=kLoop, calls=%fused_computation.22 | loop fusion | flops 696320 | bytes 1854080 | tf_op jit(solution)/shard_map/mul | solution.py:164
  (116 shorter events, 18.9 us)
Async XLA Ops:
  0.6 68.0 %copy-start = (f32[17,17]{1,0:T(8,128)S(1)}, f32[17,17]{1,0:T(8,128)}, u32[]{:S(2)}) copy-start(f32[17,17]{1,0:T(8,128)} %param.16) | copy-start | bytes 3472
  4.8 15.2 %collective-permute-start.1 = (f32[42,1,128]{2,1,0:T(1,128)S(1)}, f32[42,1,128]{2,1,0:T(1,128)S(1)}, u32[]{:S(2)}, u32[]{:S(2)}) collective-permute-start(f32[42,1,128]{2,1,0:T(1,128)S(1)} %get-tuple-element.72), channel_id=1, source_target_pairs={{2,0},{4,2},{6,4},{8,6},{10,8},{12,10},{14,12},{16,14},{18,16},{20... | collective-permute-start | bytes 64520 | tf_op jit(solution)/shard_map/ppermute | solution.py:32
  9.0 11.0 %collective-permute-start = (f32[42,1,128]{2,1,0:T(1,128)S(1)}, f32[42,1,128]{2,1,0:T(1,128)S(1)}, u32[]{:S(2)}, u32[]{:S(2)}) collective-permute-start(f32[42,1,128]{2,1,0:T(1,128)S(1)} %get-tuple-element.71), channel_id=1, source_target_pairs={{0,2},{2,4},{4,6},{6,8},{8,10},{10,12},{12,14},{14,16},{16,18},{18... | collective-permute-start | bytes 64520 | tf_op jit(solution)/shard_map/ppermute | solution.py:30
  12.3 39.5 %collective-permute-start.9 = (f32[136,2,128]{2,1,0:T(2,128)S(1)}, f32[136,2,128]{2,1,0:T(2,128)S(1)}, u32[]{:S(2)}, u32[]{:S(2)}) collective-permute-start(f32[136,2,128]{2,1,0:T(2,128)S(1)} %get-tuple-element.60), channel_id=1, source_target_pairs={{2,0},{4,2},{6,4},{8,6},{10,8},{12,10},{14,12},{16,14},{18,16},{20... | collective-permute-start | bytes 417800 | tf_op jit(solution)/shard_map/ppermute | solution.py:32
  18.0 33.8 %collective-permute-start.8 = (f32[136,2,128]{2,1,0:T(2,128)S(1)}, f32[136,2,128]{2,1,0:T(2,128)S(1)}, u32[]{:S(2)}, u32[]{:S(2)}) collective-permute-start(f32[136,2,128]{2,1,0:T(2,128)S(1)} %get-tuple-element.59), channel_id=1, source_target_pairs={{0,2},{2,4},{4,6},{6,8},{8,10},{10,12},{12,14},{14,16},{16,18},{18... | collective-permute-start | bytes 417800 | tf_op jit(solution)/shard_map/ppermute | solution.py:30
  20.2 4.5 %collective-permute-start.3 = (f32[42,10,1]{2,1,0:T(8,128)S(1)}, f32[42,10,1]{2,1,0:T(8,128)S(1)}, u32[]{:S(2)}, u32[]{:S(2)}) collective-permute-start(f32[42,10,1]{2,1,0:T(8,128)S(1)} %get-tuple-element.62), channel_id=1, source_target_pairs={{1,0},{3,2},{5,4},{7,6},{9,8},{11,10},{13,12},{15,14},{17,16},{19,... | collective-permute-start | bytes 5048 | tf_op jit(solution)/shard_map/ppermute | solution.py:32
  21.5 4.3 %collective-permute-start.2 = (f32[42,10,1]{2,1,0:T(8,128)S(1)}, f32[42,10,1]{2,1,0:T(8,128)S(1)}, u32[]{:S(2)}, u32[]{:S(2)}) collective-permute-start(f32[42,10,1]{2,1,0:T(8,128)S(1)} %get-tuple-element.61), channel_id=1, source_target_pairs={{0,1},{2,3},{4,5},{6,7},{8,9},{10,11},{12,13},{14,15},{16,17},{18,... | collective-permute-start | bytes 5048 | tf_op jit(solution)/shard_map/ppermute | solution.py:30
  26.9 1.7 %copy-start.18 = (s32[8,128]{1,0:T(8,128)S(1)}, s32[8,128]{1,0:T(8,128)}, u32[]{:S(2)}) copy-start(s32[8,128]{1,0:T(8,128)} %param.13) | copy-start | bytes 12292
  26.9 1.7 %copy-start.19 = (s32[8,128]{1,0:T(8,128)S(1)}, s32[8,128]{1,0:T(8,128)}, u32[]{:S(2)}) copy-start(s32[8,128]{1,0:T(8,128)} %param.14) | copy-start | bytes 12292
  28.7 7.9 %collective-permute-start.5 = (f32[34,2,128]{2,1,0:T(2,128)S(1)}, f32[34,2,128]{2,1,0:T(2,128)S(1)}, u32[]{:S(2)}, u32[]{:S(2)}) collective-permute-start(f32[34,2,128]{2,1,0:T(2,128)S(1)} %get-tuple-element.74), channel_id=1, source_target_pairs={{2,0},{4,2},{6,4},{8,6},{10,8},{12,10},{14,12},{16,14},{18,16},{20... | collective-permute-start | bytes 104456 | tf_op jit(solution)/shard_map/ppermute | solution.py:32
  34.4 7.6 %collective-permute-start.4 = (f32[34,2,128]{2,1,0:T(2,128)S(1)}, f32[34,2,128]{2,1,0:T(2,128)S(1)}, u32[]{:S(2)}, u32[]{:S(2)}) collective-permute-start(f32[34,2,128]{2,1,0:T(2,128)S(1)} %get-tuple-element.73), channel_id=1, source_target_pairs={{0,2},{2,4},{4,6},{6,8},{8,10},{10,12},{12,14},{14,16},{16,18},{18... | collective-permute-start | bytes 104456 | tf_op jit(solution)/shard_map/ppermute | solution.py:30
  36.5 13.4 %copy-start.11 = (f32[2,8,10,130]{3,2,1,0:T(8,128)}, f32[2,8,10,130]{3,2,1,0:T(8,128)S(1)}, u32[]{:S(2)}) copy-start(f32[2,8,10,130]{3,2,1,0:T(8,128)S(1)} %add_multiply_fusion) | copy-start | bytes 249604
  42.3 5.7 %collective-permute-start.7 = (f32[34,12,2]{2,1,0:T(8,128)S(1)}, f32[34,12,2]{2,1,0:T(8,128)S(1)}, u32[]{:S(2)}, u32[]{:S(2)}) collective-permute-start(f32[34,12,2]{2,1,0:T(8,128)S(1)} %get-tuple-element.66), channel_id=1, source_target_pairs={{1,0},{3,2},{5,4},{7,6},{9,8},{11,10},{13,12},{15,14},{17,16},{19,... | collective-permute-start | bytes 9800 | tf_op jit(solution)/shard_map/ppermute | solution.py:32
  43.6 4.4 %collective-permute-start.6 = (f32[34,12,2]{2,1,0:T(8,128)S(1)}, f32[34,12,2]{2,1,0:T(8,128)S(1)}, u32[]{:S(2)}, u32[]{:S(2)}) collective-permute-start(f32[34,12,2]{2,1,0:T(8,128)S(1)} %get-tuple-element.65), channel_id=1, source_target_pairs={{0,1},{2,3},{4,5},{6,7},{8,9},{10,11},{12,13},{14,15},{16,17},{18,... | collective-permute-start | bytes 9800 | tf_op jit(solution)/shard_map/ppermute | solution.py:30
  48.4 3.4 %copy-start.1 = (f32[17,8,8,128]{3,2,1,0:T(8,128)S(1)}, f32[17,8,8,128]{3,2,1,0:T(8,128)}, u32[]{:S(2)}) copy-start(f32[17,8,8,128]{3,2,1,0:T(8,128)} %param.12) | copy-start | bytes 1671172
  50.1 8.3 %copy-start.2 = (f32[8,10,130]{2,1,0:T(8,128)}, f32[8,10,130]{2,1,0:T(8,128)S(1)}, u32[]{:S(2)}) copy-start(f32[8,10,130]{2,1,0:T(8,128)S(1)} %slice.473) | copy-start | bytes 124804
  52.9 8.1 %collective-permute-start.11 = (f32[136,12,2]{0,2,1:T(2,128)S(1)}, f32[136,12,2]{0,2,1:T(2,128)S(1)}, u32[]{:S(2)}, u32[]{:S(2)}) collective-permute-start(f32[136,12,2]{0,2,1:T(2,128)S(1)} %copy.15), channel_id=1, source_target_pairs={{1,0},{3,2},{5,4},{7,6},{9,8},{11,10},{13,12},{15,14},{17,16},{19,... | collective-permute-start | bytes 39176 | tf_op jit(solution)/shard_map/ppermute | solution.py:32
  54.7 6.8 %collective-permute-start.10 = (f32[136,12,2]{0,2,1:T(2,128)S(1)}, f32[136,12,2]{0,2,1:T(2,128)}, u32[]{:S(2)}, u32[]{:S(2)}) collective-permute-start(f32[136,12,2]{0,2,1:T(2,128)S(1)} %copy.14), channel_id=1, source_target_pairs={{0,1},{2,3},{4,5},{6,7},{8,9},{10,11},{12,13},{14,15},{16,17},{18,... | collective-permute-start | bytes 39176 | tf_op jit(solution)/shard_map/ppermute | solution.py:30
  62.9 1.6 %copy-start.10 = (f32[8,12,132]{2,1,0:T(8,128)S(1)}, f32[8,12,132]{2,1,0:T(8,128)}, u32[]{:S(2)}) copy-start(f32[8,12,132]{2,1,0:T(8,128)} %get-tuple-element.58) | copy-start | bytes 152068
  62.9 2.3 %copy-start.9 = (f32[8,12,132]{2,1,0:T(8,128)S(1)}, f32[8,12,132]{2,1,0:T(8,128)}, u32[]{:S(2)}) copy-start(f32[8,12,132]{2,1,0:T(8,128)} %get-tuple-element.44) | copy-start | bytes 152068
  62.9 2.3 %copy-start.15 = (pred[8,12,132]{2,1,0:T(8,128)(4,1)S(1)}, pred[8,12,132]{2,1,0:T(8,128)(4,1)}, u32[]{:S(2)}) copy-start(pred[8,12,132]{2,1,0:T(8,128)(4,1)} %get-tuple-element.17) | copy-start | bytes 38020
  62.9 2.3 %copy-start.16 = (pred[8,12,132]{2,1,0:T(8,128)(4,1)S(1)}, pred[8,12,132]{2,1,0:T(8,128)(4,1)}, u32[]{:S(2)}) copy-start(pred[8,12,132]{2,1,0:T(8,128)(4,1)} %get-tuple-element.43) | copy-start | bytes 38020
  70.1 3.4 %copy-start.4 = (f32[8,12,132]{2,1,0:T(8,128)S(1)}, f32[8,12,132]{2,1,0:T(8,128)}, u32[]{:S(2)}) copy-start(f32[8,12,132]{2,1,0:T(8,128)} %get-tuple-element.81) | copy-start | bytes 152068
  71.0 3.6 %copy-start.3 = (f32[8,10,130]{2,1,0:T(8,128)S(1)}, f32[8,10,130]{2,1,0:T(8,128)}, u32[]{:S(2)}) copy-start(f32[8,10,130]{2,1,0:T(8,128)} %copy-done.2) | copy-start | bytes 124804
  74.6 3.0 %copy-start.5 = (f32[8,10,130]{2,1,0:T(8,128)S(1)}, f32[8,10,130]{2,1,0:T(8,128)}, u32[]{:S(2)}) copy-start(f32[8,10,130]{2,1,0:T(8,128)} %get-tuple-element.12) | copy-start | bytes 124804
  74.6 3.0 %copy-start.6 = (f32[8,10,130]{2,1,0:T(8,128)S(1)}, f32[8,10,130]{2,1,0:T(8,128)}, u32[]{:S(2)}) copy-start(f32[8,10,130]{2,1,0:T(8,128)} %get-tuple-element.46) | copy-start | bytes 124804
  74.6 3.0 %copy-start.7 = (f32[8,10,130]{2,1,0:T(8,128)S(1)}, f32[8,10,130]{2,1,0:T(8,128)}, u32[]{:S(2)}) copy-start(f32[8,10,130]{2,1,0:T(8,128)} %get-tuple-element.67) | copy-start | bytes 124804
  74.6 3.0 %copy-start.8 = (f32[8,10,130]{2,1,0:T(8,128)S(1)}, f32[8,10,130]{2,1,0:T(8,128)}, u32[]{:S(2)}) copy-start(f32[8,10,130]{2,1,0:T(8,128)} %get-tuple-element.68) | copy-start | bytes 124804
  74.6 3.0 %copy-start.13 = (pred[8,10,130]{2,1,0:T(8,128)(4,1)S(1)}, pred[8,10,130]{2,1,0:T(8,128)(4,1)}, u32[]{:S(2)}) copy-start(pred[8,10,130]{2,1,0:T(8,128)(4,1)} %get-tuple-element.11) | copy-start | bytes 31204
  74.6 3.0 %copy-start.14 = (pred[8,10,130]{2,1,0:T(8,128)(4,1)S(1)}, pred[8,10,130]{2,1,0:T(8,128)(4,1)}, u32[]{:S(2)}) copy-start(pred[8,10,130]{2,1,0:T(8,128)(4,1)} %get-tuple-element.45) | copy-start | bytes 31204
  82.0 4.9 %copy-start.17 = (f32[1,8,8,128]{3,2,1,0:T(8,128)S(1)}, f32[1,8,8,128]{3,2,1,0:T(8,128)}, u32[]{:S(2)}) copy-start(f32[1,8,8,128]{3,2,1,0:T(8,128)} %slice.472) | copy-start | bytes 98308
  82.4 5.4 %copy-start.12 = (f32[8,8,128]{2,1,0:T(8,128)S(1)}, f32[8,8,128]{2,1,0:T(8,128)}, u32[]{:S(2)}) copy-start(f32[8,8,128]{2,1,0:T(8,128)} %slice.497) | copy-start | bytes 98308
where the time goes:
time: 91.3 us; the launch traced here: 90.5 us
  starting transfers between devices  35.1 us (38%)
  other arithmetic  24.7 us (27%)
  local copies, waits for them, and re-layouts  19.7 us (22%)
  waiting for transfers between devices  6.68 us (7%)
  matrix products  2.99 us (3%)
  between operations  1.39 us (2%)
    ppermute x6, starting transfers between devices, with_halo(): lax.ppermute(head, axis, [((i + 1) % count, i) for i in range(ends)])  19.6 us
    ppermute x6, starting transfers between devices, with_halo(): lax.ppermute(tail, axis, [(i, (i + 1) % count) for i in range(ends)])  15.5 us
    ppermute x6, waiting for transfers between devices, with_halo(): lax.ppermute(tail, axis, [(i, (i + 1) % count) for i in range(ends)])  6.66 us
    mul x2, other arithmetic, tracer_step(): return wet_cells * (advected + sub_step * change)  5.72 us
    slice x4, local copies, waits for them, and re-layouts, tracer_step(): coupled[2:]  5.06 us
    concatenate x6, other arithmetic, with_halo(): jnp.concatenate([lax.ppermute(tail, axis, [(i, (i + 1) % count) for i in...  2.81 us
    sub x2, other arithmetic, tracer_step(): tracers - sub_step * (flux_x - shifted(flux_x, 0, -1) + flux_y - shifted(...  2.63 us
    mul x2, other arithmetic, tracer_step(): diffuse_x = wet_east * 0.5 * (kappa + shifted(kappa, 0, 1))  2.59 us
  transfers between devices with their start and end apart: 12, of which 2 were waited for; matrix products, arithmetic and copies ran while one was open for 15% of the time, Pallas kernels for 0%

commit v1 on v0

v1 whole, which is shorter than its diff:
```python
import functools

import jax
import jax.numpy as jnp
from jax import lax
from jax.experimental import pallas as pl
from jax.experimental.pallas import tpu as pltpu
from jax.sharding import PartitionSpec as P

NSUB = 2
heat_coef = 0.2
salt_coef = 0.25
gravity = 0.3
viscosity = 0.1
coriolis_coef = 0.3
tracer_diff = 0.1
kappa_base = 0.02
kappa_var = 0.1
water_att = 0.1
chlorophyll_att = 0.2
heat_gain = 1.0
MESH = pl.DeviceIdType.MESH


def growth_of(biome, growth, row, kinds):
    value = jnp.float32(0.0)
    for kind in range(kinds):
        value = jnp.where(biome[row] == kind, growth[kind], value)
    return value


def write_misc(misc, land, bottom, biome, growth, rows, cols, kinds):
    misc[0:rows, :] = (land[...] * bottom[...]).astype(jnp.float32)
    for row in range(rows):
        misc[rows + row : rows + row + 1, :] = jnp.full(
            (1, cols), growth_of(biome, growth, row, kinds), jnp.float32
        )


def exchange(sizes, biome, growth, vel, thick, hydro, tracers, land, bottom, *refs):
    lats, lons, layers, rows, cols, kinds, near, sides = sizes
    fields = tracers.shape[0] // rows
    got_ns = refs[0]
    got_lon = [refs[1 + 6 * i : 7 + 6 * i] for i in range(sides)]
    misc, pack, send_ns, recv_ns, send_lon, recv_lon = refs[1 + 6 * sides :]
    lat, lon = lax.axis_index("lat"), lax.axis_index("lon")
    barrier = pltpu.get_barrier_semaphore()
    around = [
        (lat > 0, (lat - 1, lon)),
        (lat < lats - 1, (lat + 1, lon)),
        (lon > 0, (lat, lon - 1)),
        (lon < lons - 1, (lat, lon + 1)),
    ]
    for there, where in around:

        @pl.when(there)
        def _(where=where):
            pl.semaphore_signal(barrier, inc=1, device_id=where, device_id_type=MESH)

    write_misc(misc, land, bottom, biome, growth, rows, cols, kinds)

    def state_row(side, start, row):
        for ref, count in ((vel, 2 * layers), (thick, layers), (hydro, 2 * layers)):
            pack[side, start : start + count, :] = ref[pl.ds(row, count, stride=rows), :]
            start += count

    def tracer_row(side, start, row):
        pack[side, start : start + fields, :] = tracers[pl.ds(row, fields, stride=rows), :]

    state = 5 * layers
    for side in range(2):
        order = (rows - 1, rows - 2, rows - 3) if side == 0 else (0, 1, 2)
        state_row(side, 0, order[0])
        tracer_row(side, state, order[0])
        state_row(side, state + fields, order[1])
        pack[side, 2 * state + fields : near, :] = misc[...]
        tracer_row(side, near, order[1])
        state_row(side, near + fields, order[2])

    peers = sum(there.astype(jnp.int32) for there, _ in around)
    pl.semaphore_wait(barrier, peers)

    def ns_copy(side):
        to = lat + 1 if side == 0 else lat - 1
        return pltpu.make_async_remote_copy(
            src_ref=pack.at[side],
            dst_ref=got_ns.at[side],
            send_sem=send_ns.at[side],
            recv_sem=recv_ns.at[side],
            device_id=(to, lon),
            device_id_type=MESH,
        )

    def lon_copy(way, item):
        slot = way if sides == 2 else 0
        to = lon + 1 if way == 0 else lon - 1
        if item < 5:
            src = (vel, thick, hydro, tracers, misc)[item]
            dst = got_lon[slot][item]
        else:
            src = got_ns.at[item - 5, 0:near]
            dst = got_lon[slot][5].at[item - 5]
        return pltpu.make_async_remote_copy(
            src_ref=src,
            dst_ref=dst,
            send_sem=send_lon.at[way, item],
            recv_sem=recv_lon.at[way, item],
            device_id=(lat, to),
            device_id_type=MESH,
        )

    south, north = lat > 0, lat < lats - 1
    west, east = lon > 0, lon < lons - 1
    ns_send = (north, south)
    ns_recv = (south, north)
    lon_send = (east, west)
    lon_recv = (west, east)
    for side in range(2):

        @pl.when(ns_send[side])
        def _(side=side):
            ns_copy(side).start()

    for way in range(2):

        @pl.when(lon_send[way])
        def _(way=way):
            for item in range(5):
                lon_copy(way, item).start()

    for side in range(2):

        @pl.when(ns_recv[side])
        def _(side=side):
            ns_copy(side).wait_recv()
            for way in range(2):

                @pl.when(lon_send[way])
                def _(way=way):
                    lon_copy(way, 5 + side).start()

    for way in range(2):

        @pl.when(lon_recv[way])
        def _(way=way):
            for item in range(5):
                lon_copy(way, item).wait_recv()
            for side in range(2):

                @pl.when(ns_recv[side])
                def _(side=side):
                    lon_copy(way, 5 + side).wait_recv()

        @pl.when(lon_send[way])
        def _(way=way):
            for item in range(5):
                lon_copy(way, item).wait_send()
            for side in range(2):

                @pl.when(ns_recv[side])
                def _(side=side):
                    lon_copy(way, 5 + side).wait_send()

    for side in range(2):

        @pl.when(ns_send[side])
        def _(side=side):
            ns_copy(side).wait_send()


def to_east(values):
    return pltpu.roll(values, values.shape[-1] - 1, values.ndim - 1)


def to_west(values):
    return pltpu.roll(values, 1, values.ndim - 1)


def compute(sizes, biome, growth, vel, thick, hydro, tracers, land, bottom, rates, *refs):
    lats, lons, layers, rows, cols, kinds, near, sides = sizes
    fields = tracers.shape[0] // rows
    ntr = fields // layers
    got_ns = refs[0]
    got_lon = [refs[1 + 6 * i : 7 + 6 * i] for i in range(sides)]
    out_vel, out_thick, out_hydro, out_tr, out_abs = refs[1 + 6 * sides : 6 + 6 * sides]
    misc, st, tr, mid, depth, grow, coef, glow, wets = refs[6 + 6 * sides :]
    lat, lon = lax.axis_index("lat"), lax.axis_index("lon")
    span = 2 * cols
    state = 5 * layers
    write_misc(misc, land, bottom, biome, growth, rows, cols, kinds)

    lanes = lax.broadcasted_iota(jnp.int32, (1, cols), 1)
    first = lanes < cols // 2
    lane_e = jnp.logical_and(first, lon < lons - 1)
    lane_w = jnp.logical_and(jnp.logical_not(first), lon > 0)

    def beside(load, mask=None):
        west_part = load(got_lon[0])
        east_part = load(got_lon[-1])
        use_e, use_w = lane_e, lane_w
        if mask is not None:
            use_e, use_w = jnp.logical_and(use_e, mask), jnp.logical_and(use_w, mask)
        return jnp.where(use_e, east_part, jnp.where(use_w, west_part, 0.0))

    def both(ref, at, start, own, side_values):
        count = own.shape[0]
        ref[at, start : start + count, 0:cols] = own
        ref[at, start : start + count, cols:span] = side_values

    for row in range(rows):
        start = 0
        for item, (ref, count) in enumerate(
            ((vel, 2 * layers), (thick, layers), (hydro, 2 * layers))
        ):
            pick = pl.ds(row, count, stride=rows)
            both(
                st, 3 + row, start, ref[pick, :], beside(lambda got, i=item, p=pick: got[i][p, :])
            )
            start += count
        pick = pl.ds(row, fields, stride=rows)
        both(tr, 2 + row, 0, tracers[pick, :], beside(lambda got, p=pick: got[3][p, :]))
    for ref, begin in ((depth, 0), (grow, rows)):
        for row in range(rows):
            pick = slice(begin + row, begin + row + 1)
            ref[3 + row, :, 0:cols] = jnp.broadcast_to(misc[pick, :], (layers, cols))
            ref[3 + row, :, cols:span] = jnp.broadcast_to(
                beside(lambda got, p=pick: got[4][p, :]), (layers, cols)
            )
    for side in range(2):
        there = lat > 0 if side == 0 else lat < lats - 1
        mask = jnp.logical_and(lanes >= 0, there)

        def own_part(begin, count, side=side, mask=mask):
            return jnp.where(mask, got_ns[side, begin : begin + count, :], 0.0)

        def far_part(begin, count, side=side, mask=mask):
            return beside(lambda got: got[5][side, begin : begin + count, :], mask)

        place = (2, 1, 0) if side == 0 else (rows + 3, rows + 4, rows + 5)
        place_tr = (1, 0) if side == 0 else (rows + 2, rows + 3)
        source = (rows - 1, rows - 2, rows - 3) if side == 0 else (0, 1, 2)
        both(st, place[0], 0, own_part(0, state), far_part(0, state))
        both(tr, place_tr[0], 0, own_part(state, fields), far_part(state, fields))
        both(st, place[1], 0, own_part(state + fields, state), far_part(state + fields, state))
        both(tr, place_tr[1], 0, own_part(near, fields), jnp.zeros((fields, cols), jnp.float32))
        both(
            st, place[2], 0, own_part(near + fields, state), jnp.zeros((state, cols), jnp.float32)
        )
        begin = 2 * state + fields
        for ref, extra in ((depth, 0), (grow, rows)):
            for step in range(3):
                at = begin + extra + source[step]
                ref[place[step], :, 0:cols] = jnp.broadcast_to(own_part(at, 1), (layers, cols))
                ref[place[step], :, cols:span] = jnp.broadcast_to(far_part(at, 1), (layers, cols))

    total = rows * lats
    deep = rows + 6
    base = (lat * rows).astype(jnp.float32)

    def latitude(begin, count):
        at = lax.broadcasted_iota(jnp.int32, (count, layers, span), 0).astype(jnp.float32)
        return 2.0 * ((base + (at + begin)) + 0.5) / total - 1.0

    level = lax.broadcasted_iota(jnp.int32, (1, layers, span), 1)
    wet = (level.astype(jnp.float32) < depth[...]).astype(jnp.float32)
    wet_e = wet * to_east(wet)
    wet_n = wet[:-1] * wet[1:]
    u = st[:, 0:layers, :]
    v = st[:, layers : 2 * layers, :]
    h = st[:, 2 * layers : 3 * layers, :]
    warm = st[:, 3 * layers : 4 * layers, :]
    salt = st[:, 4 * layers : 5 * layers, :]

    def inner(a):
        return a[1 : deep - 1]

    def laplace(a, low, high):
        block, eface = a[low:high], wet_e[low:high]
        fe = eface * (to_east(block) - block)
        fn = wet_n[low - 1 : high] * (a[low : high + 1] - a[low - 1 : high])
        return fe - to_west(fe) + fn[1:] - fn[:-1]

    dens = salt_coef * salt - heat_coef * warm
    press = gravity * h + dens
    cor = coriolis_coef * latitude(-2.0, deep - 2)
    new_u = inner(wet_e) * (
        inner(u)
        + cor * inner(v)
        - (to_east(inner(press)) - inner(press))
        + viscosity * laplace(u, 1, deep - 1)
    )
    new_v = wet_n[1:] * (
        inner(v)
        - cor * inner(u)
        - (press[2:] - inner(press))
        + viscosity * laplace(v, 1, deep - 1)
    )
    q_e = inner(wet_e * u * 0.5 * (h + to_east(h)))
    q_n = wet_n * v[:-1] * 0.5 * (h[:-1] + h[1:])
    new_h = inner(wet) * (inner(h) - (q_e - to_west(q_e) + q_n[1:] - q_n[:-1]))
    dens = inner(dens)
    below = jnp.where(level < layers - 1, pltpu.roll(dens, layers - 1, 1) - dens, 0.0)
    kappa = inner(wet) * (kappa_base + kappa_var / (1.0 + 10.0 * below * below))

    def upwind(flow, spread):
        return jnp.maximum(flow, 0.0) + spread, jnp.minimum(flow, 0.0) - spread

    he, ke = new_h[1:-1], kappa[1:-1]
    face_e, face_n = wet_e[2:-2], wet_n[1:-1]
    a_e, b_e = upwind(
        face_e * new_u[1:-1] * 0.5 * (he + to_east(he)), face_e * 0.5 * (ke + to_east(ke))
    )
    a_n, b_n = upwind(
        face_n * new_v[:-1] * 0.5 * (new_h[:-1] + new_h[1:]),
        face_n * 0.5 * (kappa[:-1] + kappa[1:]),
    )
    sub = 1.0 / NSUB
    a_w, b_w = to_west(a_e), to_west(b_e)
    coef[0] = 1.0 - sub * (a_e - b_w + a_n[1:] - b_n[:-1])
    coef[1] = -sub * b_e
    coef[2] = sub * a_w
    coef[3] = -sub * b_n[1:]
    coef[4] = sub * a_n[:-1]
    wet_in = wet[2:-2]
    wets[...] = wet_in

    chl = tr[1 : rows + 3, layers : 2 * layers, :]
    att = wet_in * (water_att + chlorophyll_att * chl * chl)
    summed = att
    step = 1
    while step < layers:
        summed = summed + jnp.where(level >= step, pltpu.roll(summed, step, 1), 0.0)
        step *= 2
    lat_in = latitude(-1.0, rows + 2)
    top = (1.0 - 0.8 * lat_in * lat_in) * jnp.exp(att - summed)
    glow[...] = grow[2 : rows + 4] * top
    light = (top * (1.0 - jnp.exp(-att)))[1:-1, :, 0:cols]
    mine = wet[3:-3, :, 0:cols]
    mixed_t = (
        mine * (warm[3:-3] + tracer_diff * laplace(warm, 3, deep - 3))[:, :, 0:cols]
        + heat_gain * light
    )
    mixed_s = mine * (salt[3:-3] + tracer_diff * laplace(salt, 3, deep - 3))[:, :, 0:cols]
    for row in range(rows):
        pick = pl.ds(row, layers, stride=rows)
        later = pl.ds(layers * rows + row, layers, stride=rows)
        out_vel[pick, :] = new_u[2 + row, :, 0:cols]
        out_vel[later, :] = new_v[2 + row, :, 0:cols]
        out_thick[pick, :] = new_h[2 + row, :, 0:cols]
        out_hydro[pick, :] = mixed_t[row]
        out_hydro[later, :] = mixed_s[row]
        out_abs[pick, :] = light[row]

    wide = lax.broadcasted_iota(jnp.int32, (fields, ntr), 0) // layers
    pick_t = (wide == lax.broadcasted_iota(jnp.int32, (fields, ntr), 1)).astype(jnp.float32)
    spread_rates = jnp.dot(
        pick_t,
        lax.dot_general(
            rates[...],
            pick_t,
            (((1,), (1,)), ((), ())),
            precision=lax.Precision.HIGHEST,
            preferred_element_type=jnp.float32,
        ),
        precision=lax.Precision.HIGHEST,
        preferred_element_type=jnp.float32,
    )
    same = (
        lax.broadcasted_iota(jnp.int32, (fields, fields), 0) % layers
        == lax.broadcasted_iota(jnp.int32, (fields, fields), 1) % layers
    )
    couple = jnp.where(same, sub * spread_rates, 0.0)
    couple_hi = couple.astype(jnp.bfloat16)
    couple_lo = (couple - couple_hi.astype(jnp.float32)).astype(jnp.bfloat16)

    def advance(src, at, width):
        c = src[at + 1].reshape(ntr, layers, span)
        up = src[at + 2].reshape(ntr, layers, span)[:, :, 0:width]
        down = src[at].reshape(ntr, layers, span)[:, :, 0:width]
        return c, up, down

    def finish(src, at, face, width):
        c, up, down = advance(src, at, width)
        k = [coef[i, face, :, 0:width] for i in range(5)]
        adv = (
            k[0] * c[:, :, 0:width]
            + k[1] * to_east(c)[:, :, 0:width]
            + k[2] * to_west(c)[:, :, 0:width]
            + k[3] * up
            + k[4] * down
        )
        flat = adv.reshape(fields, width)
        hi = flat.astype(jnp.bfloat16)
        lo = (flat - hi.astype(jnp.float32)).astype(jnp.bfloat16)

        def mul(a, b):
            return jnp.dot(a, b, preferred_element_type=jnp.float32)

        new = flat + (mul(couple_hi, hi) + (mul(couple_hi, lo) + mul(couple_lo, hi)))
        nut, plk = adv[0], adv[1]
        uptake = glow[face, :, 0:width] * plk * nut * nut / (1.0 + nut * nut)
        new = new.reshape(ntr, layers, width)
        w = wets[face, :, 0:width]
        first_two = (
            w * (new[0] - sub * uptake),
            w * (new[1] + sub * uptake),
        )
        return (w * new).reshape(fields, width), first_two

    def first_step(at, carry):
        new, (zero, one) = finish(tr, at, at, span)
        mid[at] = new
        mid[at, 0:layers, :] = zero
        mid[at, layers : 2 * layers, :] = one
        return carry

    lax.fori_loop(0, rows + 2, first_step, 0)
    for row in range(rows):
        new, (zero, one) = finish(mid, row, row + 1, cols)
        out_tr[pl.ds(row, fields, stride=rows), :] = new
        out_tr[pl.ds(row, layers, stride=rows), :] = zero
        out_tr[pl.ds(layers * rows + row, layers, stride=rows), :] = one


def per_device(
    velocity,
    thickness,
    hydrography,
    tracers,
    land_mask,
    bottom_layer,
    row_biome,
    reaction_rates,
    growth_rates,
):
    ntr, layers, rows, cols = tracers.shape
    lats, lons = lax.axis_size("lat"), lax.axis_size("lon")
    state, fields = 5 * layers, ntr * layers
    near = 2 * state + fields + 2 * rows
    whole = near + fields + state
    sides = 1 if lons <= 2 else 2
    sizes = (lats, lons, layers, rows, cols, growth_rates.shape[0], near, sides)
    flat = [a.reshape(-1, cols) for a in (velocity, thickness, hydrography, tracers)]
    vmem = pl.BlockSpec(memory_space=pltpu.VMEM)
    smem = pl.BlockSpec(memory_space=pltpu.SMEM)
    f32 = jnp.float32
    lon_shapes = [jax.ShapeDtypeStruct(a.shape, f32) for a in flat] + [
        jax.ShapeDtypeStruct((2 * rows, cols), f32),
        jax.ShapeDtypeStruct((2, near, cols), f32),
    ]
    got = pl.pallas_call(
        functools.partial(exchange, sizes),
        out_shape=[jax.ShapeDtypeStruct((2, whole, cols), f32)] + lon_shapes * sides,
        in_specs=[smem] * 2 + [vmem] * 6,
        out_specs=[pl.BlockSpec(memory_space=pl.ANY)] * (1 + 6 * sides),
        scratch_shapes=[
            pltpu.VMEM((2 * rows, cols), f32),
            pltpu.VMEM((2, whole, cols), f32),
            pltpu.SemaphoreType.DMA((2,)),
            pltpu.SemaphoreType.DMA((2,)),
            pltpu.SemaphoreType.DMA((2, 7)),
            pltpu.SemaphoreType.DMA((2, 7)),
        ],
        compiler_params=pltpu.CompilerParams(
            collective_id=0, has_side_effects=True, vmem_limit_bytes=16 * 1024 * 1024
        ),
        name="exchange",
    )(row_biome, growth_rates, *flat, land_mask, bottom_layer)
    span = 2 * cols
    outs = pl.pallas_call(
        functools.partial(compute, sizes),
        out_shape=[jax.ShapeDtypeStruct(flat[i].shape, f32) for i in (0, 1, 2, 3, 1)],
        in_specs=[smem] * 2 + [vmem] * (7 + 1 + 6 * sides),
        out_specs=[vmem] * 5,
        scratch_shapes=[
            pltpu.VMEM((2 * rows, cols), f32),
            pltpu.VMEM((rows + 6, state, span), f32),
            pltpu.VMEM((rows + 4, fields, span), f32),
            pltpu.VMEM((rows + 2, fields, span), f32),
            pltpu.VMEM((rows + 6, layers, span), f32),
            pltpu.VMEM((rows + 6, layers, span), f32),
            pltpu.VMEM((5, rows + 2, layers, span), f32),
            pltpu.VMEM((rows + 2, layers, span), f32),
            pltpu.VMEM((rows + 2, layers, span), f32),
        ],
        compiler_params=pltpu.CompilerParams(vmem_limit_bytes=32 * 1024 * 1024),
        name="ocean_step",
    )(row_biome, growth_rates, *flat, land_mask, bottom_layer, reaction_rates, *got)
    return (
        outs[0].reshape(velocity.shape),
        outs[1].reshape(thickness.shape),
        outs[2].reshape(hydrography.shape),
        outs[3].reshape(tracers.shape),
        outs[4].reshape(thickness.shape),
    )


def solution(mesh):
    in_specs = (
        P(None, None, "lat", "lon"),
        P(None, "lat", "lon"),
        P(None, None, "lat", "lon"),
        P(None, None, "lat", "lon"),
        P("lat", "lon"),
        P("lat", "lon"),
        P("lat"),
        P(),
        P(),
    )
    out_specs = (
        P(None, None, "lat", "lon"),
        P(None, "lat", "lon"),
        P(None, None, "lat", "lon"),
        P(None, None, "lat", "lon"),
        P(None, "lat", "lon"),
    )
    return jax.shard_map(
        per_device, mesh=mesh, in_specs=in_specs, out_specs=out_specs, check_vma=False
    )
```

time: 91.3 us -> 29 us (0.32)
  the two profiles are of different devices: /device:TPU:8 before, /device:TPU:0 now
where the time goes in v1:
time: 29 us; the launch traced here: 28.5 us
  Pallas kernels  22.3 us (77%)
  local copies, waits for them, and re-layouts  5.52 us (19%)
  between operations  0.72 us (2%)
    pallas_call x1, Pallas kernels, per_device(): pl.pallas_call(functools.partial(exchange, sizes), out_shape=[jax.ShapeDt...  15.6 us
    pallas_call x1, Pallas kernels, per_device(): pl.pallas_call(functools.partial(compute, sizes), out_shape=[jax.ShapeDty...  6.69 us
    unnamed x26, local copies, waits for them, and re-layouts  5.52 us

profile of v1, /device:TPU:0, one launch (start us, length us, event | category | flops | bytes accessed | tf_op | source)
XLA Modules:
  0.0 28.5 jit_solution(16660050729727616047)
XLA Ops:
  0.6 0.0 copy-start.8
  0.6 0.0 copy-start.11
  0.7 0.0 copy-start.12
  0.7 0.7 %copy-done.8 = s32[8,128]{1,0:T(8,128)S(1)} copy-done((s32[8,128]{1,0:T(8,128)S(1)}, s32[8,128]{1,0:T(8,128)}, u32[]{:S(2)}) %copy-start.8) | copy-done | bytes 4120
  1.3 0.0 copy-done.11
  1.3 0.0 copy-done.12
  1.3 0.0 copy-start
  1.3 1.1 %copy-done = f32[17,8,8,128]{3,2,1,0:T(8,128)S(1)} copy-done((f32[17,8,8,128]{3,2,1,0:T(8,128)S(1)}, f32[17,8,8,128]{3,2,1,0:T(8,128)}, u32[]{:S(2)}) %copy-start) | copy-done | bytes 557080
  2.4 0.0 copy-start.2
  2.4 0.8 %copy-done.2 = f32[2,8,8,128]{3,2,1,0:T(8,128)S(1)} copy-done((f32[2,8,8,128]{3,2,1,0:T(8,128)S(1)}, f32[2,8,8,128]{3,2,1,0:T(8,128)}, u32[]{:S(2)}) %copy-start.2) | copy-done | bytes 65560
  3.2 0.0 copy-start.4
  3.2 0.8 %copy-done.4 = f32[2,8,8,128]{3,2,1,0:T(8,128)S(1)} copy-done((f32[2,8,8,128]{3,2,1,0:T(8,128)S(1)}, f32[2,8,8,128]{3,2,1,0:T(8,128)}, u32[]{:S(2)}) %copy-start.4) | copy-done | bytes 65560
  4.1 0.0 copy-start.6
  4.1 0.8 %copy-done.6 = f32[8,8,128]{2,1,0:T(8,128)S(1)} copy-done((f32[8,8,128]{2,1,0:T(8,128)S(1)}, f32[8,8,128]{2,1,0:T(8,128)}, u32[]{:S(2)}) %copy-start.6) | copy-done | bytes 32792
  4.8 0.0 copy-start.9
  4.8 0.7 %copy-done.9 = s32[8,128]{1,0:T(8,128)S(1)} copy-done((s32[8,128]{1,0:T(8,128)S(1)}, s32[8,128]{1,0:T(8,128)}, u32[]{:S(2)}) %copy-start.9) | copy-done | bytes 4120
  5.5 0.0 copy-start.1
  5.5 0.0 copy-start.3
  5.5 0.0 copy-start.5
  5.5 0.0 copy-start.7
  5.5 15.6 %exchange.1 = (f32[2,408,128]{2,1,0:T(8,128)S(1)}, f32[128,128]{1,0:T(8,128)S(1)}, f32[64,128]{1,0:T(8,128)S(1)}, f32[128,128]{1,0:T(8,128)S(1)}, f32[1088,128]{...) custom-call(s32[8]{0:T(128)S(1)} %copy-done.11, f32[4]{0:T(128)S(1)} %copy-done.12, ...), custom_call_target="tpu_custom_call" | custom-call | tf_op jit(solution)/shard_map/exchange/pallas_call | solution.py:451
  21.1 0.0 copy-start.10
  21.2 0.0 copy-done.1
  21.2 0.0 copy-done.3
  21.2 0.0 copy-done.5
  21.2 0.0 copy-done.7
  21.2 0.7 %copy-done.10 = f32[17,17]{1,0:T(8,128)S(1)} copy-done((f32[17,17]{1,0:T(8,128)S(1)}, f32[17,17]{1,0:T(8,128)}, u32[]{:S(2)}) %copy-start.10) | copy-done | bytes 1180
  21.9 6.7 %ocean_step.1 = (f32[128,128]{1,0:T(8,128)}, f32[64,128]{1,0:T(8,128)}, f32[128,128]{1,0:T(8,128)}, f32[1088,128]{1,0:T(8,128)}, f32[64,128]{1,0:T(8,128)}) custom-call(s32[8]{0:T(128)S(1)} %copy-done.11, f32[4]{0:T(128)S(1)} %copy-done.12, f32[128,128]{1,0:T(8,128)S(1)} %bitcast.12, f32[64,128]{1,0:T(8,128)S(1)} %bitcast.16, f32[128,128]{1,0:T(8,128)S(1)} %bitcast.14, ...), custom_call_target="tpu_custom_call" | custom-call | tf_op jit(solution)/shard_map/ocean_step/pallas_call | solution.py:470
Async XLA Ops:
  0.6 0.7 %copy-start.8 = (s32[8,128]{1,0:T(8,128)S(1)}, s32[8,128]{1,0:T(8,128)}, u32[]{:S(2)}) copy-start(s32[8,128]{1,0:T(8,128)} %land.3) | copy-start | bytes 12292
  0.6 0.7 %copy-start.11 = (s32[8]{0:T(128)S(1)}, s32[8]{0:T(128)}, u32[]{:S(2)}) copy-start(s32[8]{0:T(128)} %biome.3) | copy-start | bytes 100
  0.7 0.7 %copy-start.12 = (f32[4]{0:T(128)S(1)}, f32[4]{0:T(128)}, u32[]{:S(2)}) copy-start(f32[4]{0:T(128)} %growth.3) | copy-start | bytes 52
  1.3 1.1 %copy-start = (f32[17,8,8,128]{3,2,1,0:T(8,128)S(1)}, f32[17,8,8,128]{3,2,1,0:T(8,128)}, u32[]{:S(2)}) copy-start(f32[17,8,8,128]{3,2,1,0:T(8,128)} %param.12) | copy-start | bytes 1671172
  2.4 0.8 %copy-start.2 = (f32[2,8,8,128]{3,2,1,0:T(8,128)S(1)}, f32[2,8,8,128]{3,2,1,0:T(8,128)}, u32[]{:S(2)}) copy-start(f32[2,8,8,128]{3,2,1,0:T(8,128)} %param.9) | copy-start | bytes 196612
  3.2 0.8 %copy-start.4 = (f32[2,8,8,128]{3,2,1,0:T(8,128)S(1)}, f32[2,8,8,128]{3,2,1,0:T(8,128)}, u32[]{:S(2)}) copy-start(f32[2,8,8,128]{3,2,1,0:T(8,128)} %param.11) | copy-start | bytes 196612
  4.1 0.8 %copy-start.6 = (f32[8,8,128]{2,1,0:T(8,128)S(1)}, f32[8,8,128]{2,1,0:T(8,128)}, u32[]{:S(2)}) copy-start(f32[8,8,128]{2,1,0:T(8,128)} %param.10) | copy-start | bytes 98308
  4.8 0.7 %copy-start.9 = (s32[8,128]{1,0:T(8,128)S(1)}, s32[8,128]{1,0:T(8,128)}, u32[]{:S(2)}) copy-start(s32[8,128]{1,0:T(8,128)} %bottom.3) | copy-start | bytes 12292
  5.5 15.7 %copy-start.1 = (f32[17,8,8,128]{3,2,1,0:T(8,128)S(1)}, f32[17,8,8,128]{3,2,1,0:T(8,128)}, u32[]{:S(2)}) copy-start(f32[17,8,8,128]{3,2,1,0:T(8,128)} %param.12) | copy-start | bytes 1671172
  5.5 15.7 %copy-start.3 = (f32[2,8,8,128]{3,2,1,0:T(8,128)S(1)}, f32[2,8,8,128]{3,2,1,0:T(8,128)}, u32[]{:S(2)}) copy-start(f32[2,8,8,128]{3,2,1,0:T(8,128)} %param.9) | copy-start | bytes 196612
  5.5 15.7 %copy-start.5 = (f32[2,8,8,128]{3,2,1,0:T(8,128)S(1)}, f32[2,8,8,128]{3,2,1,0:T(8,128)}, u32[]{:S(2)}) copy-start(f32[2,8,8,128]{3,2,1,0:T(8,128)} %param.11) | copy-start | bytes 196612
  5.5 15.7 %copy-start.7 = (f32[8,8,128]{2,1,0:T(8,128)S(1)}, f32[8,8,128]{2,1,0:T(8,128)}, u32[]{:S(2)}) copy-start(f32[8,8,128]{2,1,0:T(8,128)} %param.10) | copy-start | bytes 98308
  21.1 0.7 %copy-start.10 = (f32[17,17]{1,0:T(8,128)S(1)}, f32[17,17]{1,0:T(8,128)}, u32[]{:S(2)}) copy-start(f32[17,17]{1,0:T(8,128)} %rates.1) | copy-start | bytes 3472

commit v2 on v1

--- a/solution.py
+++ b/solution.py
@@ -37,12 +37,20 @@
         )
 
 
-def exchange(sizes, biome, growth, vel, thick, hydro, tracers, land, bottom, *refs):
+def exchange(sizes, biome, growth, *refs):
+    held, refs = refs[:6], refs[6:]
     lats, lons, layers, rows, cols, kinds, near, sides = sizes
-    fields = tracers.shape[0] // rows
+    fields = held[3].shape[0] // rows
     got_ns = refs[0]
     got_lon = [refs[1 + 6 * i : 7 + 6 * i] for i in range(sides)]
-    misc, pack, send_ns, recv_ns, send_lon, recv_lon = refs[1 + 6 * sides :]
+    misc, pack, send_ns, recv_ns, send_lon, recv_lon, load_sem = refs[1 + 6 * sides : 8 + 6 * sides]
+    local = refs[8 + 6 * sides :]
+    vel, thick, hydro, tracers, land, bottom = local
+    loads = [
+        pltpu.make_async_copy(held[i], local[i], load_sem.at[i]) for i in (4, 5, 3, 0, 2, 1)
+    ]
+    for load in loads:
+        load.start()
     lat, lon = lax.axis_index("lat"), lax.axis_index("lon")
     barrier = pltpu.get_barrier_semaphore()
     around = [
@@ -57,12 +65,31 @@
         def _(where=where):
             pl.semaphore_signal(barrier, inc=1, device_id=where, device_id_type=MESH)
 
+    for load in loads[:2]:
+        load.wait()
     write_misc(misc, land, bottom, biome, growth, rows, cols, kinds)
+    for load in loads[2:]:
+        load.wait()
 
     def state_row(side, start, row):
         for ref, count in ((vel, 2 * layers), (thick, layers), (hydro, 2 * layers)):
             pack[side, start : start + count, :] = ref[pl.ds(row, count, stride=rows), :]
             start += count
+
+    def second_row(side, start, row):
+        flow, one = 2 * layers, layers
+        pack[side, start : start + flow, :] = vel[pl.ds(row, flow, stride=rows), :]
+        pack[side, start + flow : start + flow + one, :] = thick[pl.ds(row, one, stride=rows), :]
+        warm = hydro[pl.ds(row, one, stride=rows), :]
+        salt = hydro[pl.ds(one * rows + row, one, stride=rows), :]
+        pack[side, start + flow + one : start + flow + 2 * one, :] = (
+            salt_coef * salt - heat_coef * warm
+        )
+
+    def third_row(side, start, row):
+        one = layers
+        pack[side, start : start + one, :] = vel[pl.ds(one * rows + row, one, stride=rows), :]
+        pack[side, start + one : start + 2 * one, :] = thick[pl.ds(row, one, stride=rows), :]
 
     def tracer_row(side, start, row):
         pack[side, start : start + fields, :] = tracers[pl.ds(row, fields, stride=rows), :]
@@ -72,21 +99,21 @@
         order = (rows - 1, rows - 2, rows - 3) if side == 0 else (0, 1, 2)
         state_row(side, 0, order[0])
         tracer_row(side, state, order[0])
-        state_row(side, state + fields, order[1])
-        pack[side, 2 * state + fields : near, :] = misc[...]
+        second_row(side, state + fields, order[1])
+        pack[side, near - 2 * rows : near, :] = misc[...]
         tracer_row(side, near, order[1])
-        state_row(side, near + fields, order[2])
+        third_row(side, near + fields, order[2])
 
     peers = sum(there.astype(jnp.int32) for there, _ in around)
     pl.semaphore_wait(barrier, peers)
 
-    def ns_copy(side):
+    def ns_copy(side, part):
         to = lat + 1 if side == 0 else lat - 1
         return pltpu.make_async_remote_copy(
-            src_ref=pack.at[side],
-            dst_ref=got_ns.at[side],
-            send_sem=send_ns.at[side],
-            recv_sem=recv_ns.at[side],
+            src_ref=pack.at[side, cuts[part] : cuts[part + 1]],
+            dst_ref=got_ns.at[side, cuts[part] : cuts[part + 1]],
+            send_sem=send_ns.at[side, part],
+            recv_sem=recv_ns.at[side, part],
             device_id=(to, lon),
             device_id_type=MESH,
         )
@@ -95,7 +122,7 @@
         slot = way if sides == 2 else 0
         to = lon + 1 if way == 0 else lon - 1
         if item < 5:
-            src = (vel, thick, hydro, tracers, misc)[item]
+            src = (*held[:4], misc)[item]
             dst = got_lon[slot][item]
         else:
             src = got_ns.at[item - 5, 0:near]
@@ -109,17 +136,19 @@
             device_id_type=MESH,
         )
 
+    cuts = (0, near, got_ns.shape[1])
     south, north = lat > 0, lat < lats - 1
     west, east = lon > 0, lon < lons - 1
     ns_send = (north, south)
     ns_recv = (south, north)
     lon_send = (east, west)
     lon_recv = (west, east)
-    for side in range(2):
-
-        @pl.when(ns_send[side])
-        def _(side=side):
-            ns_copy(side).start()
+    for part in range(2):
+        for side in range(2):
+
+            @pl.when(ns_send[side])
+            def _(side=side, part=part):
+                ns_copy(side, part).start()
 
     for way in range(2):
 
@@ -132,7 +161,7 @@
 
         @pl.when(ns_recv[side])
         def _(side=side):
-            ns_copy(side).wait_recv()
+            ns_copy(side, 0).wait_recv()
             for way in range(2):
 
                 @pl.when(lon_send[way])
@@ -163,9 +192,14 @@
 
     for side in range(2):
 
+        @pl.when(ns_recv[side])
+        def _(side=side):
+            ns_copy(side, 1).wait_recv()
+
         @pl.when(ns_send[side])
         def _(side=side):
-            ns_copy(side).wait_send()
+            ns_copy(side, 0).wait_send()
+            ns_copy(side, 1).wait_send()
 
 
 def to_east(values):
@@ -174,6 +208,17 @@
 
 def to_west(values):
     return pltpu.roll(values, 1, values.ndim - 1)
+
+
+def load_all(body, count, biome, growth, *refs):
+    held, outs = refs[:count], refs[count : count + 5]
+    local, rest, sems = refs[count + 5 : 2 * count + 5], refs[2 * count + 5 : -1], refs[-1]
+    loads = [pltpu.make_async_copy(held[i], local[i], sems.at[i]) for i in range(count)]
+    for load in loads:
+        load.start()
+    for load in loads:
+        load.wait()
+    body(biome, growth, *local, *outs, *rest)
 
 
 def compute(sizes, biome, growth, vel, thick, hydro, tracers, land, bottom, rates, *refs):
@@ -241,12 +286,25 @@
         source = (rows - 1, rows - 2, rows - 3) if side == 0 else (0, 1, 2)
         both(st, place[0], 0, own_part(0, state), far_part(0, state))
         both(tr, place_tr[0], 0, own_part(state, fields), far_part(state, fields))
-        both(st, place[1], 0, own_part(state + fields, state), far_part(state + fields, state))
+        both(
+            st,
+            place[1],
+            0,
+            own_part(state + fields, 3 * layers),
+            far_part(state + fields, 3 * layers),
+        )
+        empty = jnp.zeros((layers, cols), jnp.float32)
+        at = state + fields + 3 * layers
+        both(st, place[1], 3 * layers, empty, empty)
+        scale = 1.0 / salt_coef
+        both(
+            st, place[1], 4 * layers, scale * own_part(at, layers), scale * far_part(at, layers)
+        )
         both(tr, place_tr[1], 0, own_part(near, fields), jnp.zeros((fields, cols), jnp.float32))
-        both(
-            st, place[2], 0, own_part(near + fields, state), jnp.zeros((state, cols), jnp.float32)
-        )
-        begin = 2 * state + fields
+        nothing = jnp.zeros((state, cols), jnp.float32)
+        both(st, place[2], 0, nothing, nothing)
+        st[place[2], layers : 3 * layers, 0:cols] = own_part(near + fields, 2 * layers)
+        begin = near - 2 * rows
         for ref, extra in ((depth, 0), (grow, rows)):
             for step in range(3):
                 at = begin + extra + source[step]
@@ -436,13 +494,14 @@
     ntr, layers, rows, cols = tracers.shape
     lats, lons = lax.axis_size("lat"), lax.axis_size("lon")
     state, fields = 5 * layers, ntr * layers
-    near = 2 * state + fields + 2 * rows
-    whole = near + fields + state
+    near = state + fields + 4 * layers + 2 * rows
+    whole = near + fields + 2 * layers
     sides = 1 if lons <= 2 else 2
     sizes = (lats, lons, layers, rows, cols, growth_rates.shape[0], near, sides)
     flat = [a.reshape(-1, cols) for a in (velocity, thickness, hydrography, tracers)]
     vmem = pl.BlockSpec(memory_space=pltpu.VMEM)
     smem = pl.BlockSpec(memory_space=pltpu.SMEM)
+    hbm = pl.BlockSpec(memory_space=pltpu.HBM)
     f32 = jnp.float32
     lon_shapes = [jax.ShapeDtypeStruct(a.shape, f32) for a in flat] + [
         jax.ShapeDtypeStruct((2 * rows, cols), f32),
@@ -451,28 +510,35 @@
     got = pl.pallas_call(
         functools.partial(exchange, sizes),
         out_shape=[jax.ShapeDtypeStruct((2, whole, cols), f32)] + lon_shapes * sides,
-        in_specs=[smem] * 2 + [vmem] * 6,
+        in_specs=[smem] * 2 + [hbm] * 6,
         out_specs=[pl.BlockSpec(memory_space=pl.ANY)] * (1 + 6 * sides),
         scratch_shapes=[
             pltpu.VMEM((2 * rows, cols), f32),
             pltpu.VMEM((2, whole, cols), f32),
-            pltpu.SemaphoreType.DMA((2,)),
-            pltpu.SemaphoreType.DMA((2,)),
+            pltpu.SemaphoreType.DMA((2, 2)),
+            pltpu.SemaphoreType.DMA((2, 2)),
             pltpu.SemaphoreType.DMA((2, 7)),
             pltpu.SemaphoreType.DMA((2, 7)),
+            pltpu.SemaphoreType.DMA((6,)),
+            *[pltpu.VMEM(a.shape, f32) for a in flat],
+            pltpu.VMEM((rows, cols), jnp.int32),
+            pltpu.VMEM((rows, cols), jnp.int32),
         ],
         compiler_params=pltpu.CompilerParams(
-            collective_id=0, has_side_effects=True, vmem_limit_bytes=16 * 1024 * 1024
+            collective_id=0, has_side_effects=True, vmem_limit_bytes=62 * 1024 * 1024
         ),
         name="exchange",
     )(row_biome, growth_rates, *flat, land_mask, bottom_layer)
     span = 2 * cols
+    operands = [*flat, land_mask, bottom_layer, reaction_rates, *got]
+    count = len(operands)
     outs = pl.pallas_call(
-        functools.partial(compute, sizes),
+        functools.partial(load_all, functools.partial(compute, sizes), count),
         out_shape=[jax.ShapeDtypeStruct(flat[i].shape, f32) for i in (0, 1, 2, 3, 1)],
-        in_specs=[smem] * 2 + [vmem] * (7 + 1 + 6 * sides),
+        in_specs=[smem] * 2 + [hbm] * count,
         out_specs=[vmem] * 5,
-        scratch_shapes=[
+        scratch_shapes=[pltpu.VMEM(a.shape, a.dtype) for a in operands]
+        + [
             pltpu.VMEM((2 * rows, cols), f32),
             pltpu.VMEM((rows + 6, state, span), f32),
             pltpu.VMEM((rows + 4, fields, span), f32),
@@ -482,10 +548,11 @@
             pltpu.VMEM((5, rows + 2, layers, span), f32),
             pltpu.VMEM((rows + 2, layers, span), f32),
             pltpu.VMEM((rows + 2, layers, span), f32),
+            pltpu.SemaphoreType.DMA((count,)),
         ],
-        compiler_params=pltpu.CompilerParams(vmem_limit_bytes=32 * 1024 * 1024),
+        compiler_params=pltpu.CompilerParams(vmem_limit_bytes=62 * 1024 * 1024),
         name="ocean_step",
-    )(row_biome, growth_rates, *flat, land_mask, bottom_layer, reaction_rates, *got)
+    )(row_biome, growth_rates, *operands)
     return (
         outs[0].reshape(velocity.shape),
         outs[1].reshape(thickness.shape),

time: 29 us -> 23.7 us (0.82)
  local copies, waits for them, and re-layouts: 5.52 us -> 0 us
  Pallas kernels: 22.3 us -> 22.8 us
    unnamed x26 -> x0, local copies, waits for them, and re-layouts: 5.52 us -> none
    pallas_call x1, Pallas kernels: 6.69 us -> 8.58 us  [per_device(): pl.pallas_call(functools.partial(load_all, functools.partial(compute, siz...]
    pallas_call x1, Pallas kernels: 15.6 us -> 14.3 us  [per_device(): pl.pallas_call(functools.partial(exchange, sizes), out_shape=[jax.ShapeDt...]
where the time goes in v2:
time: 23.7 us; the launch traced here: 23.5 us
  Pallas kernels  22.8 us (96%)
  between operations  0.64 us (3%)
    pallas_call x1, Pallas kernels, per_device(): pl.pallas_call(functools.partial(exchange, sizes), out_shape=[jax.ShapeDt...  14.3 us
    pallas_call x1, Pallas kernels, per_device(): pl.pallas_call(functools.partial(load_all, functools.partial(compute, siz...  8.58 us

profile of v2, /device:TPU:0, one launch (start us, length us, event | category | flops | bytes accessed | tf_op | source)
XLA Modules:
  0.0 23.5 jit_solution(12595530513246780444)
XLA Ops:
  0.6 14.3 %exchange.1 = (f32[2,376,128]{2,1,0:T(8,128)}, f32[128,128]{1,0:T(8,128)}, f32[64,128]{1,0:T(8,128)}, f32[128,128]{1,0:T(8,128)}, f32[1088,128]{1,0:T(8,128)}, /...) custom-call(s32[8]{0:T(128)} %biome.3, f32[4]{0:T(128)} %growth.3, f32[128,128]{1,0:T(8,128)} %bitcast.11, f32[64,128]{1,0:T(8,128)} %bitcast.15, ...), custom_call_target="tpu_custom_call" | custom-call | tf_op jit(solution)/shard_map/exchange/pallas_call | solution.py:510
  14.9 8.6 %ocean_step.1 = (f32[128,128]{1,0:T(8,128)}, f32[64,128]{1,0:T(8,128)}, f32[128,128]{1,0:T(8,128)}, f32[1088,128]{1,0:T(8,128)}, f32[64,128]{1,0:T(8,128)}) custom-call(s32[8]{0:T(128)} %biome.3, f32[4]{0:T(128)} %growth.3, f32[128,128]{1,0:T(8,128)} %bitcast.12, f32[64,128]{1,0:T(8,128)} %bitcast.16, f32[128,128]{1,0:T(8,128)} %bitcast.14, ...), custom_call_target="tpu_custom_call" | custom-call | tf_op jit(solution)/shard_map/ocean_step/pallas_call | solution.py:535

commit v3 on v2

--- a/solution.py
+++ b/solution.py
@@ -216,12 +216,10 @@
     loads = [pltpu.make_async_copy(held[i], local[i], sems.at[i]) for i in range(count)]
     for load in loads:
         load.start()
-    for load in loads:
-        load.wait()
-    body(biome, growth, *local, *outs, *rest)
-
-
-def compute(sizes, biome, growth, vel, thick, hydro, tracers, land, bottom, rates, *refs):
+    body(loads, biome, growth, *local, *outs, *rest)
+
+
+def compute(sizes, loads, biome, growth, vel, thick, hydro, tracers, land, bottom, rates, *refs):
     lats, lons, layers, rows, cols, kinds, near, sides = sizes
     fields = tracers.shape[0] // rows
     ntr = fields // layers
@@ -232,7 +230,15 @@
     lat, lon = lax.axis_index("lat"), lax.axis_index("lon")
     span = 2 * cols
     state = 5 * layers
+    for load in loads[:7]:
+        load.wait()
     write_misc(misc, land, bottom, biome, growth, rows, cols, kinds)
+    for row in range(rows):
+        start = 0
+        for ref, count in ((vel, 2 * layers), (thick, layers), (hydro, 2 * layers)):
+            st[3 + row, start : start + count, 0:cols] = ref[pl.ds(row, count, stride=rows), :]
+            start += count
+        tr[2 + row, :, 0:cols] = tracers[pl.ds(row, fields, stride=rows), :]
 
     lanes = lax.broadcasted_iota(jnp.int32, (1, cols), 1)
     first = lanes < cols // 2
@@ -252,18 +258,40 @@
         ref[at, start : start + count, 0:cols] = own
         ref[at, start : start + count, cols:span] = side_values
 
+    wide = lax.broadcasted_iota(jnp.int32, (fields, ntr), 0) // layers
+    pick_t = (wide == lax.broadcasted_iota(jnp.int32, (fields, ntr), 1)).astype(jnp.float32)
+    spread_rates = jnp.dot(
+        pick_t,
+        lax.dot_general(
+            rates[...],
+            pick_t,
+            (((1,), (1,)), ((), ())),
+            precision=lax.Precision.HIGHEST,
+            preferred_element_type=jnp.float32,
+        ),
+        precision=lax.Precision.HIGHEST,
+        preferred_element_type=jnp.float32,
+    )
+    same = (
+        lax.broadcasted_iota(jnp.int32, (fields, fields), 0) % layers
+        == lax.broadcasted_iota(jnp.int32, (fields, fields), 1) % layers
+    )
+    couple = jnp.where(same, spread_rates / NSUB, 0.0)
+    couple_hi = couple.astype(jnp.bfloat16)
+    couple_lo = (couple - couple_hi.astype(jnp.float32)).astype(jnp.bfloat16)
+
+    for load in loads[7:]:
+        load.wait()
     for row in range(rows):
         start = 0
-        for item, (ref, count) in enumerate(
-            ((vel, 2 * layers), (thick, layers), (hydro, 2 * layers))
-        ):
+        for item, count in enumerate((2 * layers, layers, 2 * layers)):
             pick = pl.ds(row, count, stride=rows)
-            both(
-                st, 3 + row, start, ref[pick, :], beside(lambda got, i=item, p=pick: got[i][p, :])
+            st[3 + row, start : start + count, cols:span] = beside(
+                lambda got, i=item, p=pick: got[i][p, :]
             )
             start += count
         pick = pl.ds(row, fields, stride=rows)
-        both(tr, 2 + row, 0, tracers[pick, :], beside(lambda got, p=pick: got[3][p, :]))
+        tr[2 + row, :, cols:span] = beside(lambda got, p=pick: got[3][p, :])
     for ref, begin in ((depth, 0), (grow, rows)):
         for row in range(rows):
             pick = slice(begin + row, begin + row + 1)
@@ -409,28 +437,6 @@
         out_hydro[later, :] = mixed_s[row]
         out_abs[pick, :] = light[row]
 
-    wide = lax.broadcasted_iota(jnp.int32, (fields, ntr), 0) // layers
-    pick_t = (wide == lax.broadcasted_iota(jnp.int32, (fields, ntr), 1)).astype(jnp.float32)
-    spread_rates = jnp.dot(
-        pick_t,
-        lax.dot_general(
-            rates[...],
-            pick_t,
-            (((1,), (1,)), ((), ())),
-            precision=lax.Precision.HIGHEST,
-            preferred_element_type=jnp.float32,
-        ),
-        precision=lax.Precision.HIGHEST,
-        preferred_element_type=jnp.float32,
-    )
-    same = (
-        lax.broadcasted_iota(jnp.int32, (fields, fields), 0) % layers
-        == lax.broadcasted_iota(jnp.int32, (fields, fields), 1) % layers
-    )
-    couple = jnp.where(same, sub * spread_rates, 0.0)
-    couple_hi = couple.astype(jnp.bfloat16)
-    couple_lo = (couple - couple_hi.astype(jnp.float32)).astype(jnp.bfloat16)
-
     def advance(src, at, width):
         c = src[at + 1].reshape(ntr, layers, span)
         up = src[at + 2].reshape(ntr, layers, span)[:, :, 0:width]
@@ -465,14 +471,14 @@
         )
         return (w * new).reshape(fields, width), first_two
 
-    def first_step(at, carry):
+    def first_step(at):
         new, (zero, one) = finish(tr, at, at, span)
         mid[at] = new
         mid[at, 0:layers, :] = zero
         mid[at, layers : 2 * layers, :] = one
-        return carry
-
-    lax.fori_loop(0, rows + 2, first_step, 0)
+
+    for at in range(rows + 2):
+        first_step(at)
     for row in range(rows):
         new, (zero, one) = finish(mid, row, row + 1, cols)
         out_tr[pl.ds(row, fields, stride=rows), :] = new

time: 23.7 us -> 21.4 us (0.903)
  Pallas kernels: 22.8 us -> 20.6 us
    pallas_call x1, Pallas kernels: 8.58 us -> 6.29 us  [per_device(): pl.pallas_call(functools.partial(load_all, functools.partial(compute, siz...]
where the time goes in v3:
time: 21.4 us; the launch traced here: 21.2 us
  Pallas kernels  20.6 us (96%)
  between operations  0.64 us (3%)
    pallas_call x1, Pallas kernels, per_device(): pl.pallas_call(functools.partial(exchange, sizes), out_shape=[jax.ShapeDt...  14.3 us
    pallas_call x1, Pallas kernels, per_device(): pl.pallas_call(functools.partial(load_all, functools.partial(compute, siz...  6.29 us

profile of v3, /device:TPU:0, one launch (start us, length us, event | category | flops | bytes accessed | tf_op | source)
XLA Modules:
  0.0 21.2 jit_solution(7854191383019227775)
XLA Ops:
  0.6 14.3 %exchange.1 = (f32[2,376,128]{2,1,0:T(8,128)}, f32[128,128]{1,0:T(8,128)}, f32[64,128]{1,0:T(8,128)}, f32[128,128]{1,0:T(8,128)}, f32[1088,128]{1,0:T(8,128)}, /...) custom-call(s32[8]{0:T(128)} %biome.3, f32[4]{0:T(128)} %growth.3, f32[128,128]{1,0:T(8,128)} %bitcast.11, f32[64,128]{1,0:T(8,128)} %bitcast.15, ...), custom_call_target="tpu_custom_call" | custom-call | tf_op jit(solution)/shard_map/exchange/pallas_call | solution.py:516
  14.9 6.3 %ocean_step.1 = (f32[128,128]{1,0:T(8,128)}, f32[64,128]{1,0:T(8,128)}, f32[128,128]{1,0:T(8,128)}, f32[1088,128]{1,0:T(8,128)}, f32[64,128]{1,0:T(8,128)}) custom-call(s32[8]{0:T(128)} %biome.3, f32[4]{0:T(128)} %growth.3, f32[128,128]{1,0:T(8,128)} %bitcast.12, f32[64,128]{1,0:T(8,128)} %bitcast.16, f32[128,128]{1,0:T(8,128)} %bitcast.14, ...), custom_call_target="tpu_custom_call" | custom-call | tf_op jit(solution)/shard_map/ocean_step/pallas_call | solution.py:541

commit v4 on v3

--- a/solution.py
+++ b/solution.py
@@ -65,48 +65,6 @@
         def _(where=where):
             pl.semaphore_signal(barrier, inc=1, device_id=where, device_id_type=MESH)
 
-    for load in loads[:2]:
-        load.wait()
-    write_misc(misc, land, bottom, biome, growth, rows, cols, kinds)
-    for load in loads[2:]:
-        load.wait()
-
-    def state_row(side, start, row):
-        for ref, count in ((vel, 2 * layers), (thick, layers), (hydro, 2 * layers)):
-            pack[side, start : start + count, :] = ref[pl.ds(row, count, stride=rows), :]
-            start += count
-
-    def second_row(side, start, row):
-        flow, one = 2 * layers, layers
-        pack[side, start : start + flow, :] = vel[pl.ds(row, flow, stride=rows), :]
-        pack[side, start + flow : start + flow + one, :] = thick[pl.ds(row, one, stride=rows), :]
-        warm = hydro[pl.ds(row, one, stride=rows), :]
-        salt = hydro[pl.ds(one * rows + row, one, stride=rows), :]
-        pack[side, start + flow + one : start + flow + 2 * one, :] = (
-            salt_coef * salt - heat_coef * warm
-        )
-
-    def third_row(side, start, row):
-        one = layers
-        pack[side, start : start + one, :] = vel[pl.ds(one * rows + row, one, stride=rows), :]
-        pack[side, start + one : start + 2 * one, :] = thick[pl.ds(row, one, stride=rows), :]
-
-    def tracer_row(side, start, row):
-        pack[side, start : start + fields, :] = tracers[pl.ds(row, fields, stride=rows), :]
-
-    state = 5 * layers
-    for side in range(2):
-        order = (rows - 1, rows - 2, rows - 3) if side == 0 else (0, 1, 2)
-        state_row(side, 0, order[0])
-        tracer_row(side, state, order[0])
-        second_row(side, state + fields, order[1])
-        pack[side, near - 2 * rows : near, :] = misc[...]
-        tracer_row(side, near, order[1])
-        third_row(side, near + fields, order[2])
-
-    peers = sum(there.astype(jnp.int32) for there, _ in around)
-    pl.semaphore_wait(barrier, peers)
-
     def ns_copy(side, part):
         to = lat + 1 if side == 0 else lat - 1
         return pltpu.make_async_remote_copy(
@@ -143,19 +101,69 @@
     ns_recv = (south, north)
     lon_send = (east, west)
     lon_recv = (west, east)
-    for part in range(2):
-        for side in range(2):
-
-            @pl.when(ns_send[side])
-            def _(side=side, part=part):
-                ns_copy(side, part).start()
-
+    peers = sum(there.astype(jnp.int32) for there, _ in around)
+    pl.semaphore_wait(barrier, peers)
     for way in range(2):
 
         @pl.when(lon_send[way])
         def _(way=way):
-            for item in range(5):
+            for item in (3, 0, 2, 1):
                 lon_copy(way, item).start()
+
+    for load in loads[:2]:
+        load.wait()
+    write_misc(misc, land, bottom, biome, growth, rows, cols, kinds)
+    for way in range(2):
+
+        @pl.when(lon_send[way])
+        def _(way=way):
+            lon_copy(way, 4).start()
+
+    for load in loads[2:]:
+        load.wait()
+
+    def state_row(side, start, row):
+        for ref, count in ((vel, 2 * layers), (thick, layers), (hydro, 2 * layers)):
+            pack[side, start : start + count, :] = ref[pl.ds(row, count, stride=rows), :]
+            start += count
+
+    def second_row(side, start, row):
+        flow, one = 2 * layers, layers
+        pack[side, start : start + flow, :] = vel[pl.ds(row, flow, stride=rows), :]
+        pack[side, start + flow : start + flow + one, :] = thick[pl.ds(row, one, stride=rows), :]
+        warm = hydro[pl.ds(row, one, stride=rows), :]
+        salt = hydro[pl.ds(one * rows + row, one, stride=rows), :]
+        pack[side, start + flow + one : start + flow + 2 * one, :] = (
+            salt_coef * salt - heat_coef * warm
+        )
+
+    def third_row(side, start, row):
+        one = layers
+        pack[side, start : start + one, :] = vel[pl.ds(one * rows + row, one, stride=rows), :]
+        pack[side, start + one : start + 2 * one, :] = thick[pl.ds(row, one, stride=rows), :]
+
+    def tracer_row(side, start, row):
+        pack[side, start : start + fields, :] = tracers[pl.ds(row, fields, stride=rows), :]
+
+    state = 5 * layers
+    order = ((rows - 1, rows - 2, rows - 3), (0, 1, 2))
+    for side in range(2):
+        state_row(side, 0, order[side][0])
+        tracer_row(side, state, order[side][0])
+        second_row(side, state + fields, order[side][1])
+        pack[side, near - 2 * rows : near, :] = misc[...]
+
+        @pl.when(ns_send[side])
+        def _(side=side):
+            ns_copy(side, 0).start()
+
+    for side in range(2):
+        tracer_row(side, near, order[side][1])
+        third_row(side, near + fields, order[side][2])
+
+        @pl.when(ns_send[side])
+        def _(side=side):
+            ns_copy(side, 1).start()
 
     for side in range(2):
 

time: 21.4 us -> 21.4 us (level)
  no operation moved by 1% of the time
where the time goes in v4:
time: 21.4 us; the launch traced here: 21.2 us
  Pallas kernels  20.6 us (96%)
  between operations  0.64 us (3%)
    pallas_call x1, Pallas kernels, per_device(): pl.pallas_call(functools.partial(exchange, sizes), out_shape=[jax.ShapeDt...  14.3 us
    pallas_call x1, Pallas kernels, per_device(): pl.pallas_call(functools.partial(load_all, functools.partial(compute, siz...  6.29 us

profile of v4, /device:TPU:0, one launch (start us, length us, event | category | flops | bytes accessed | tf_op | source)
XLA Modules:
  0.0 21.2 jit_solution(16048133172655948758)
XLA Ops:
  0.6 14.3 %exchange.1 = (f32[2,376,128]{2,1,0:T(8,128)}, f32[128,128]{1,0:T(8,128)}, f32[64,128]{1,0:T(8,128)}, f32[128,128]{1,0:T(8,128)}, f32[1088,128]{1,0:T(8,128)}, /...) custom-call(s32[8]{0:T(128)} %biome.3, f32[4]{0:T(128)} %growth.3, f32[128,128]{1,0:T(8,128)} %bitcast.11, f32[64,128]{1,0:T(8,128)} %bitcast.15, ...), custom_call_target="tpu_custom_call" | custom-call | tf_op jit(solution)/shard_map/exchange/pallas_call | solution.py:524
  15.0 6.3 %ocean_step.1 = (f32[128,128]{1,0:T(8,128)}, f32[64,128]{1,0:T(8,128)}, f32[128,128]{1,0:T(8,128)}, f32[1088,128]{1,0:T(8,128)}, f32[64,128]{1,0:T(8,128)}) custom-call(s32[8]{0:T(128)} %biome.3, f32[4]{0:T(128)} %growth.3, f32[128,128]{1,0:T(8,128)} %bitcast.12, f32[64,128]{1,0:T(8,128)} %bitcast.16, f32[128,128]{1,0:T(8,128)} %bitcast.14, ...), custom_call_target="tpu_custom_call" | custom-call | tf_op jit(solution)/shard_map/ocean_step/pallas_call | solution.py:549
